TPU v7x, 256 devices: a whole 4x4x8 slice. The times are simulated.
256 devices in a mesh: fsdp: 16 (over y_hi, x, core), seq: 16 (over z, y_lo).
Axes of the slice: x: 4, y: 4 (y_hi: 2, y_lo: 2; y = y_hi * 2 + y_lo), z: 8, core: 2. Of those that a mesh axis runs over, the one named last changes fastest.
Arguments:
- queries: bfloat16 [16, 2048, 4096], P('fsdp', 'seq'), may hold values from -8 to 8
- key_states: bfloat16 [16, 2048, 4096], P('fsdp', 'seq'), may hold values from -8 to 8
- value_states: bfloat16 [16, 2048, 4096], P('fsdp', 'seq'), may hold values from -6 to 6
- query_tangent: bfloat16 [16, 2048, 4096], P('fsdp', 'seq'), may hold values from -6 to 6
- key_tangent: bfloat16 [16, 2048, 4096], P('fsdp', 'seq'), may hold values from -6 to 6
- value_tangent: bfloat16 [16, 2048, 4096], P('fsdp', 'seq'), may hold values from -6 to 6
- gate_table: float32 [1024, 4096], P('fsdp'), may hold values from 0.5 to 1.5
- rate_table: float32 [1024, 4096], P('fsdp'), may hold values from -4 to 4
- timesteps: int32 [16, 2], replicated, may hold values from 0 to 1023
- lengths: int32 [16, 2], P('fsdp'), may hold values from 512 to 1536, as said below
Outputs:
- attended: bfloat16 [16, 2048, 4096], P('fsdp', 'seq')
- attended_tangent: bfloat16 [16, 2048, 4096], P('fsdp', 'seq')
Inputs may be any that keep to these rules, and one draw needn't show every extreme that they name: Each pack's two lengths sum to 2048.
All inputs are finite; a program needn't handle non-finite values.
Results may differ from a plain program's by a relative error of at most 0.0076.
Values may be sent and summed in bfloat16 or wider, within the bound.
No kernel may reach another device: no remote copies, remote signals or barrier semaphores. Data moves between devices by JAX's collectives and lax.ppermute only.
A program may use at most 128 MiB of HBM per device.

v0:
```python
import math

import jax
import jax.numpy as jnp
from jax import lax
from jax.sharding import PartitionSpec as P

HDIM = 128


def primal_block(query_rows, row_sample, key_rows, value_rows, key_sample, score_scale):
    scores = (
        jnp.einsum("qd,kd->qk", query_rows, key_rows, preferred_element_type=jnp.float32)
        * score_scale
    )
    same_sample = row_sample[:, None] == key_sample[None, :]
    scores = jnp.where(same_sample, scores, -jnp.inf)
    row_max = jnp.max(scores, axis=1, keepdims=True)
    exp_scores = jnp.exp(scores - row_max)
    weights = (exp_scores / jnp.sum(exp_scores, axis=1, keepdims=True)).astype(jnp.bfloat16)
    output = jnp.dot(weights, value_rows, preferred_element_type=jnp.float32).astype(jnp.bfloat16)
    return (output, weights)


def tangent_block(
    weights, query_rows, tangent_rows, key_rows, key_moves, value_rows, value_moves, score_scale
):
    score_tangent = jnp.einsum(
        "qd,kd->qk", tangent_rows, key_rows, preferred_element_type=jnp.float32
    )
    score_tangent = (
        score_tangent
        + jnp.einsum("qd,kd->qk", query_rows, key_moves, preferred_element_type=jnp.float32)
    ) * score_scale
    weights_wide = lax.optimization_barrier(weights).astype(jnp.float32)
    centre = jnp.sum(weights_wide * score_tangent, axis=1, keepdims=True)
    weight_tangent = (weights_wide * (score_tangent - centre)).astype(jnp.bfloat16)
    result = jnp.dot(weight_tangent, value_rows, preferred_element_type=jnp.float32)
    result = result + jnp.dot(weights, value_moves, preferred_element_type=jnp.float32)
    return result.astype(jnp.bfloat16)


def to_heads(array):
    return jnp.moveaxis(array[:, 0], 1, 0)


def from_heads(array):
    return jnp.moveaxis(array, 0, 1)[:, None]


def on_device(
    queries,
    key_states,
    value_states,
    query_tangent,
    key_tangent,
    value_tangent,
    gate_table,
    rate_table,
    timesteps,
    lengths,
):
    tokens = queries.shape[1]
    feature_width = queries.shape[2]
    groups = lax.axis_size("seq")
    heads_here = feature_width // (groups * HDIM)
    seq_length = tokens * groups
    block_rows = min(512, seq_length)
    block_count = seq_length // block_rows
    score_scale = 1.0 / math.sqrt(HDIM)
    first_len = lengths[0, 0]
    sample_id = (jnp.arange(seq_length, dtype=jnp.int32) >= first_len).astype(jnp.int32)
    sample_blocks = sample_id.reshape(block_count, block_rows)

    def split_heads(array):
        return array.reshape(tokens, groups, heads_here, HDIM)

    def in_blocks(array):
        return array.reshape(block_count, block_rows, HDIM)

    def both_head(head_args):
        head_q, head_k, head_v, head_qt, head_kt, head_vt = head_args

        def one_block(pieces):
            query_rows, tangent_rows, row_sample = pieces
            output, weights = primal_block(
                query_rows, row_sample, head_k, head_v, sample_id, score_scale
            )
            moved = tangent_block(
                weights, query_rows, tangent_rows, head_k, head_kt, head_v, head_vt, score_scale
            )
            return (output, moved)

        output, moved = lax.map(one_block, (in_blocks(head_q), in_blocks(head_qt), sample_blocks))
        return (output.reshape(seq_length, HDIM), moved.reshape(seq_length, HDIM))

    items = (
        lax.all_to_all(split_heads(queries), "seq", split_axis=1, concat_axis=0, tiled=True),
        lax.all_to_all(split_heads(key_states), "seq", split_axis=1, concat_axis=0, tiled=True),
        lax.all_to_all(split_heads(value_states), "seq", split_axis=1, concat_axis=0, tiled=True),
        lax.all_to_all(split_heads(query_tangent), "seq", split_axis=1, concat_axis=0, tiled=True),
        lax.all_to_all(split_heads(key_tangent), "seq", split_axis=1, concat_axis=0, tiled=True),
        lax.all_to_all(split_heads(value_tangent), "seq", split_axis=1, concat_axis=0, tiled=True),
    )
    head_arrays = tuple((to_heads(array) for array in items))
    output, moved = lax.map(both_head, head_arrays)
    attention = from_heads(output)
    attention_tangent = from_heads(moved)
    back, back_tangent = (
        lax.all_to_all(attention, "seq", split_axis=0, concat_axis=1, tiled=True),
        lax.all_to_all(attention_tangent, "seq", split_axis=0, concat_axis=1, tiled=True),
    )
    plain_rows = back.reshape(tokens, feature_width).astype(jnp.float32)
    moved_rows = back_tangent.reshape(tokens, feature_width).astype(jnp.float32)
    steps_here = gate_table.shape[0]
    offset = lax.axis_index("fsdp") * steps_here
    wanted = timesteps.reshape(-1) - offset
    one_hot = (wanted[:, None] == jnp.arange(steps_here, dtype=jnp.int32)[None, :]).astype(
        jnp.float32
    )
    gate_picks = jnp.dot(one_hot, gate_table, precision=lax.Precision.HIGHEST).reshape(
        timesteps.shape[0], timesteps.shape[1], feature_width
    )
    rate_picks = jnp.dot(one_hot, rate_table, precision=lax.Precision.HIGHEST).reshape(
        timesteps.shape[0], timesteps.shape[1], feature_width
    )
    gate_mine, rate_mine = (
        lax.psum_scatter(gate_picks, "fsdp", scatter_dimension=0, tiled=True),
        lax.psum_scatter(rate_picks, "fsdp", scatter_dimension=0, tiled=True),
    )
    token_place = lax.axis_index("seq") * tokens + jnp.arange(tokens, dtype=jnp.int32)
    second = (token_place >= first_len)[:, None]
    gate_rows = jnp.where(second, gate_mine[0, 1][None, :], gate_mine[0, 0][None, :])
    rate_rows = jnp.where(second, rate_mine[0, 1][None, :], rate_mine[0, 0][None, :])
    attended = (gate_rows * plain_rows).astype(jnp.bfloat16)
    attended_tangent = (rate_rows * plain_rows + gate_rows * moved_rows).astype(jnp.bfloat16)
    return (attended[None], attended_tangent[None])


def solution(mesh):
    in_specs = (
        P("fsdp", "seq", None),
        P("fsdp", "seq", None),
        P("fsdp", "seq", None),
        P("fsdp", "seq", None),
        P("fsdp", "seq", None),
        P("fsdp", "seq", None),
        P("fsdp", None),
        P("fsdp", None),
        P(),
        P("fsdp", None),
    )
    out_specs = (P("fsdp", "seq", None), P("fsdp", "seq", None))
    return jax.shard_map(
        on_device, mesh=mesh, in_specs=in_specs, out_specs=out_specs, check_vma=False
    )
```

profile of v0, /device:TPU:5, one launch (start us, length us, event | category | flops | bytes accessed | tf_op | source)
XLA Modules:
  0.0 524.0 jit_solution(11513514960392806338)
XLA Ops:
  10.2 9.3 %all-to-all-start = ((bf16[128,16,2,128]{3,0,2,1:T(8,128)(2,1)}), bf16[128,16,2,128]{3,0,2,1:T(8,128)(2,1)S(1)}, u32[]{:S(2)}, u32[]{:S(2)}) async-start(bf16[128,16,2,128]{3,0,2,1:T(8,128)(2,1)} %copy.37), calls=%async_computation | async-start | bytes 2097152 | tf_op jit(solution)/shard_map/all_to_all | solution.py:98
  22.5 22.4 %all-to-all-done = bf16[128,16,2,128]{3,0,2,1:T(8,128)(2,1)S(1)} async-done(((bf16[128,16,2,128]{3,0,2,1:T(8,128)(2,1)}), bf16[128,16,2,128]{3,0,2,1:T(8,128)(2,1)S(1)}, u32[]{:S(2)}, u32[]{:S(2)}) %all-to-all-start) | async-done | bytes 1048608 | tf_op jit(solution)/shard_map/all_to_all | solution.py:98
  44.8 6.4 %all-to-all-start.1 = ((bf16[128,16,2,128]{3,0,2,1:T(8,128)(2,1)}), bf16[128,16,2,128]{3,0,2,1:T(8,128)(2,1)S(1)}, u32[]{:S(2)}, u32[]{:S(2)}) async-start(bf16[128,16,2,128]{3,0,2,1:T(8,128)(2,1)} %copy.40), calls=%async_computation.1 | async-start | bytes 2097152 | tf_op jit(solution)/shard_map/all_to_all | solution.py:101
  55.7 19.9 %all-to-all-done.1 = bf16[128,16,2,128]{3,0,2,1:T(8,128)(2,1)S(1)} async-done(((bf16[128,16,2,128]{3,0,2,1:T(8,128)(2,1)}), bf16[128,16,2,128]{3,0,2,1:T(8,128)(2,1)S(1)}, u32[]{:S(2)}, u32[]{:S(2)}) %all-to-all-start.1) | async-done | bytes 1048608 | tf_op jit(solution)/shard_map/all_to_all | solution.py:101
  75.6 7.2 %all-to-all-start.2 = ((bf16[128,16,2,128]{3,0,2,1:T(8,128)(2,1)}), bf16[128,16,2,128]{3,0,2,1:T(8,128)(2,1)}, u32[]{:S(2)}, u32[]{:S(2)}) async-start(bf16[128,16,2,128]{3,0,2,1:T(8,128)(2,1)} %copy.43), calls=%async_computation.2 | async-start | bytes 2097152 | tf_op jit(solution)/shard_map/all_to_all | solution.py:99
  87.4 20.0 %all-to-all-done.2 = bf16[128,16,2,128]{3,0,2,1:T(8,128)(2,1)} async-done(((bf16[128,16,2,128]{3,0,2,1:T(8,128)(2,1)}), bf16[128,16,2,128]{3,0,2,1:T(8,128)(2,1)}, u32[]{:S(2)}, u32[]{:S(2)}) %all-to-all-start.2) | async-done | bytes 1048608 | tf_op jit(solution)/shard_map/all_to_all | solution.py:99
  107.4 7.3 %all-to-all-start.3 = ((bf16[128,16,2,128]{3,0,2,1:T(8,128)(2,1)}), bf16[128,16,2,128]{3,0,2,1:T(8,128)(2,1)}, u32[]{:S(2)}, u32[]{:S(2)}) async-start(bf16[128,16,2,128]{3,0,2,1:T(8,128)(2,1)} %copy.46), calls=%async_computation.3 | async-start | bytes 2097152 | tf_op jit(solution)/shard_map/all_to_all | solution.py:100
  119.2 20.0 %all-to-all-done.3 = bf16[128,16,2,128]{3,0,2,1:T(8,128)(2,1)} async-done(((bf16[128,16,2,128]{3,0,2,1:T(8,128)(2,1)}), bf16[128,16,2,128]{3,0,2,1:T(8,128)(2,1)}, u32[]{:S(2)}, u32[]{:S(2)}) %all-to-all-start.3) | async-done | bytes 1048608 | tf_op jit(solution)/shard_map/all_to_all | solution.py:100
  139.2 7.3 %all-to-all-start.4 = ((bf16[128,16,2,128]{3,0,2,1:T(8,128)(2,1)}), bf16[128,16,2,128]{3,0,2,1:T(8,128)(2,1)}, u32[]{:S(2)}, u32[]{:S(2)}) async-start(bf16[128,16,2,128]{3,0,2,1:T(8,128)(2,1)} %copy.49), calls=%async_computation.4 | async-start | bytes 2097152 | tf_op jit(solution)/shard_map/all_to_all | solution.py:102
  151.0 19.9 %all-to-all-done.4 = bf16[128,16,2,128]{3,0,2,1:T(8,128)(2,1)} async-done(((bf16[128,16,2,128]{3,0,2,1:T(8,128)(2,1)}), bf16[128,16,2,128]{3,0,2,1:T(8,128)(2,1)}, u32[]{:S(2)}, u32[]{:S(2)}) %all-to-all-start.4) | async-done | bytes 1048608 | tf_op jit(solution)/shard_map/all_to_all | solution.py:102
  170.9 7.3 %all-to-all-start.5 = ((bf16[128,16,2,128]{3,0,2,1:T(8,128)(2,1)}), bf16[128,16,2,128]{3,0,2,1:T(8,128)(2,1)}, u32[]{:S(2)}, u32[]{:S(2)}) async-start(bf16[128,16,2,128]{3,0,2,1:T(8,128)(2,1)} %copy.52), calls=%async_computation.5 | async-start | bytes 2097152 | tf_op jit(solution)/shard_map/all_to_all | solution.py:103
  187.3 15.4 %all-to-all-done.5 = bf16[128,16,2,128]{3,0,2,1:T(8,128)(2,1)} async-done(((bf16[128,16,2,128]{3,0,2,1:T(8,128)(2,1)}), bf16[128,16,2,128]{3,0,2,1:T(8,128)(2,1)}, u32[]{:S(2)}, u32[]{:S(2)}) %all-to-all-start.5) | async-done | bytes 1048608 | tf_op jit(solution)/shard_map/all_to_all | solution.py:103
  205.0 100.2 %while.29 = (s32[]{:T(128)}, bf16[2,2048,128]{2,1,0:T(8,128)(2,1)}, bf16[2,2048,128]{2,1,0:T(8,128)(2,1)}, bf16[2,2048,128]{2,1,0:T(8,128)(2,1)}, bf16[2,2048,12...) while((s32[]{:T(128)}, bf16[2,2048,128]{2,1,0:T(8,128)(2,1)}, ...), condition=%wide.region_7.8_spmd.clone.clone, body=%wide.region_1.7_spmd.clone.clone.sunk | while | flops 1629694464 | bytes 60994012 | solution.py:106
  211.3 41.6 %while.30 = (s32[]{:T(128)}, bf16[4,512,128]{2,1,0:T(8,128)(2,1)}, bf16[4,512,128]{2,1,0:T(8,128)(2,1)}, s32[4,512]{1,0:T(4,128)S(1)}, s32[2048]{0:T(1024)S(1)},...) while((s32[]{:T(128)}, bf16[4,512,128]{2,1,0:T(8,128)(2,1)}, ...), condition=%wide.region_6.6_spmd, body=%wide.region_2.0_spmd.sunk | while | flops 1629682176 | bytes 44200084 | solution.py:94
  261.4 41.6 %while.30 = (s32[]{:T(128)}, bf16[4,512,128]{2,1,0:T(8,128)(2,1)}, bf16[4,512,128]{2,1,0:T(8,128)(2,1)}, s32[4,512]{1,0:T(4,128)S(1)}, s32[2048]{0:T(1024)S(1)},...) while((s32[]{:T(128)}, bf16[4,512,128]{2,1,0:T(8,128)(2,1)}, ...), condition=%wide.region_6.6_spmd, body=%wide.region_2.0_spmd.sunk | while | flops 1629682176 | bytes 44200084 | solution.py:94
  305.2 3.6 copy.60
  308.8 7.2 %all-to-all-start.7 = ((bf16[2048,1,2,128]{3,2,1,0:T(2,128)(2,1)}), bf16[2048,1,2,128]{3,2,1,0:T(2,128)(2,1)S(1)}, u32[]{:S(2)}, u32[]{:S(2)}) async-start(bf16[2048,1,2,128]{3,2,1,0:T(2,128)(2,1)} %bitcast.120), calls=%async_computation.7 | async-start | bytes 2097152 | tf_op jit(solution)/shard_map/all_to_all | solution.py:111
  317.9 3.6 copy.61
  321.5 19.3 %all-to-all-done.7 = bf16[2048,1,2,128]{3,2,1,0:T(2,128)(2,1)S(1)} async-done(((bf16[2048,1,2,128]{3,2,1,0:T(2,128)(2,1)}), bf16[2048,1,2,128]{3,2,1,0:T(2,128)(2,1)S(1)}, u32[]{:S(2)}, u32[]{:S(2)}) %all-to-all-start.7) | async-done | bytes 1048608 | tf_op jit(solution)/shard_map/all_to_all | solution.py:111
  340.8 7.0 %all-to-all-start.6 = ((bf16[2048,1,2,128]{3,2,1,0:T(2,128)(2,1)}), bf16[2048,1,2,128]{3,2,1,0:T(2,128)(2,1)}, u32[]{:S(2)}, u32[]{:S(2)}) async-start(bf16[2048,1,2,128]{3,2,1,0:T(2,128)(2,1)} %bitcast.121), calls=%async_computation.6 | async-start | bytes 2097152 | tf_op jit(solution)/shard_map/all_to_all | solution.py:110
  351.4 145.8 %all-reduce.5.cloned.1.call-done = (f32[16,2,4096]{2,1,0:T(2,128)}, f32[16,2,4096]{2,1,0:T(2,128)}) async-done(((f32[16,2,4096]{2,1,0:T(2,128)}, f32[16,2,4096]{2,1,0:T(2,128)}), (f32[16,2,4096]{2,1,0:T(2,128)}, f32[16,2,4096]{2,1,0:T(2,128)})) %all-reduce.5.cloned.1.call-update) | async-done | bytes 1048592
  502.2 2.9 reshape.341
  509.7 3.9 reshape.340
  513.6 3.5 fusion.38
  (147 shorter events, 150.4 us)
Async XLA Ops:
  7.2 309.1 %copy-start = (f32[64,4096]{1,0:T(8,128)S(1)}, f32[64,4096]{1,0:T(8,128)}, u32[]{:S(2)}) copy-start(f32[64,4096]{1,0:T(8,128)} %param.20) | copy-start | bytes 3145732
  10.2 34.6 %all-to-all-start = ((bf16[128,16,2,128]{3,0,2,1:T(8,128)(2,1)}), bf16[128,16,2,128]{3,0,2,1:T(8,128)(2,1)S(1)}, u32[]{:S(2)}, u32[]{:S(2)}) async-start(bf16[128,16,2,128]{3,0,2,1:T(8,128)(2,1)} %copy.37), calls=%async_computation | async-start | bytes 2097152 | tf_op jit(solution)/shard_map/all_to_all | solution.py:98
  44.8 30.8 %all-to-all-start.1 = ((bf16[128,16,2,128]{3,0,2,1:T(8,128)(2,1)}), bf16[128,16,2,128]{3,0,2,1:T(8,128)(2,1)S(1)}, u32[]{:S(2)}, u32[]{:S(2)}) async-start(bf16[128,16,2,128]{3,0,2,1:T(8,128)(2,1)} %copy.40), calls=%async_computation.1 | async-start | bytes 2097152 | tf_op jit(solution)/shard_map/all_to_all | solution.py:101
  75.6 31.7 %all-to-all-start.2 = ((bf16[128,16,2,128]{3,0,2,1:T(8,128)(2,1)}), bf16[128,16,2,128]{3,0,2,1:T(8,128)(2,1)}, u32[]{:S(2)}, u32[]{:S(2)}) async-start(bf16[128,16,2,128]{3,0,2,1:T(8,128)(2,1)} %copy.43), calls=%async_computation.2 | async-start | bytes 2097152 | tf_op jit(solution)/shard_map/all_to_all | solution.py:99
  107.4 31.8 %all-to-all-start.3 = ((bf16[128,16,2,128]{3,0,2,1:T(8,128)(2,1)}), bf16[128,16,2,128]{3,0,2,1:T(8,128)(2,1)}, u32[]{:S(2)}, u32[]{:S(2)}) async-start(bf16[128,16,2,128]{3,0,2,1:T(8,128)(2,1)} %copy.46), calls=%async_computation.3 | async-start | bytes 2097152 | tf_op jit(solution)/shard_map/all_to_all | solution.py:100
  139.2 31.8 %all-to-all-start.4 = ((bf16[128,16,2,128]{3,0,2,1:T(8,128)(2,1)}), bf16[128,16,2,128]{3,0,2,1:T(8,128)(2,1)}, u32[]{:S(2)}, u32[]{:S(2)}) async-start(bf16[128,16,2,128]{3,0,2,1:T(8,128)(2,1)} %copy.49), calls=%async_computation.4 | async-start | bytes 2097152 | tf_op jit(solution)/shard_map/all_to_all | solution.py:102
  170.9 31.8 %all-to-all-start.5 = ((bf16[128,16,2,128]{3,0,2,1:T(8,128)(2,1)}), bf16[128,16,2,128]{3,0,2,1:T(8,128)(2,1)}, u32[]{:S(2)}, u32[]{:S(2)}) async-start(bf16[128,16,2,128]{3,0,2,1:T(8,128)(2,1)} %copy.52), calls=%async_computation.5 | async-start | bytes 2097152 | tf_op jit(solution)/shard_map/all_to_all | solution.py:103
  180.3 24.7 %copy-start.3 = (s32[1,2]{1,0:T(1,128)S(1)}, s32[1,2]{1,0:T(1,128)}, u32[]{:S(2)}) copy-start(s32[1,2]{1,0:T(1,128)} %param.23) | copy-start | bytes 28
  205.0 6.2 %copy-start.1 = (bf16[2,2048,128]{2,1,0:T(8,128)(2,1)S(1)}, bf16[2,2048,128]{2,1,0:T(8,128)(2,1)}, u32[]{:S(2)}) copy-start(bf16[2,2048,128]{2,1,0:T(8,128)(2,1)} %get-tuple-element.470) | copy-start | bytes 3145732 | tf_op jit(solution)/shard_map/while
  205.0 6.2 %copy-start.2 = (bf16[2,2048,128]{2,1,0:T(8,128)(2,1)S(1)}, bf16[2,2048,128]{2,1,0:T(8,128)(2,1)}, u32[]{:S(2)}) copy-start(bf16[2,2048,128]{2,1,0:T(8,128)(2,1)} %get-tuple-element.471) | copy-start | bytes 3145732 | tf_op jit(solution)/shard_map/while
  255.1 6.1 %copy-start.1 = (bf16[2,2048,128]{2,1,0:T(8,128)(2,1)S(1)}, bf16[2,2048,128]{2,1,0:T(8,128)(2,1)}, u32[]{:S(2)}) copy-start(bf16[2,2048,128]{2,1,0:T(8,128)(2,1)} %get-tuple-element.470) | copy-start | bytes 3145732 | tf_op jit(solution)/shard_map/while
  255.1 6.2 %copy-start.2 = (bf16[2,2048,128]{2,1,0:T(8,128)(2,1)S(1)}, bf16[2,2048,128]{2,1,0:T(8,128)(2,1)}, u32[]{:S(2)}) copy-start(bf16[2,2048,128]{2,1,0:T(8,128)(2,1)} %get-tuple-element.471) | copy-start | bytes 3145732 | tf_op jit(solution)/shard_map/while
  305.2 10.9 %copy-start.4 = (s32[16,2]{0,1:T(2,128)S(1)}, s32[16,2]{0,1:T(2,128)}, u32[]{:S(2)}) copy-start(s32[16,2]{0,1:T(2,128)} %param.22) | copy-start | bytes 388
  308.8 31.9 %all-to-all-start.7 = ((bf16[2048,1,2,128]{3,2,1,0:T(2,128)(2,1)}), bf16[2048,1,2,128]{3,2,1,0:T(2,128)(2,1)S(1)}, u32[]{:S(2)}, u32[]{:S(2)}) async-start(bf16[2048,1,2,128]{3,2,1,0:T(2,128)(2,1)} %bitcast.120), calls=%async_computation.7 | async-start | bytes 2097152 | tf_op jit(solution)/shard_map/all_to_all | solution.py:111
  317.9 32.8 %copy-start.5 = (u32[256]{0:T(256)S(1)}, u32[256]{0:T(256)}, u32[]{:S(2)}) copy-start(u32[256]{0:T(256)} %constant.63) | copy-start | bytes 3076
  340.8 164.3 %all-to-all-start.6 = ((bf16[2048,1,2,128]{3,2,1,0:T(2,128)(2,1)}), bf16[2048,1,2,128]{3,2,1,0:T(2,128)(2,1)}, u32[]{:S(2)}, u32[]{:S(2)}) async-start(bf16[2048,1,2,128]{3,2,1,0:T(2,128)(2,1)} %bitcast.121), calls=%async_computation.6 | async-start | bytes 2097152 | tf_op jit(solution)/shard_map/all_to_all | solution.py:110
  347.8 149.4 %all-reduce.5.cloned.1.call-start = ((), (), s32[]{:S(2)}) async-start(), calls=%async_computation.8 | async-start | bytes 2097152
Sparse Core Ops, SparseCore 0:
  351.9 145.2 all-reduce.4
where the time goes:
time: 530 us; the launch traced here: 524 us
  waiting for transfers between devices  283 us (53%)
  local copies, waits for them, and re-layouts  76 us (14%)
  matrix products  73.4 us (14%)
  starting transfers between devices  58.9 us (11%)
  other arithmetic  18.4 us (3%)
  between operations  14.2 us (3%)
    unnamed x2, waiting for transfers between devices  146 us
    all_to_all x1, waiting for transfers between devices, on_device(): lax.all_to_all(split_heads(queries), 'seq', split_axis=1, concat_axis=0,...  22.4 us
    all_to_all x1, waiting for transfers between devices, on_device(): lax.all_to_all(split_heads(key_states), 'seq', split_axis=1, concat_axis=...  20 us
    all_to_all x1, waiting for transfers between devices, on_device(): lax.all_to_all(split_heads(value_states), 'seq', split_axis=1, concat_axi...  20 us
    all_to_all x1, waiting for transfers between devices, on_device(): lax.all_to_all(split_heads(query_tangent), 'seq', split_axis=1, concat_ax...  19.9 us
    all_to_all x1, waiting for transfers between devices, on_device(): lax.all_to_all(split_heads(key_tangent), 'seq', split_axis=1, concat_axis...  19.9 us
    all_to_all x1, waiting for transfers between devices, on_device(): lax.all_to_all(attention_tangent, 'seq', split_axis=0, concat_axis=1, til...  19.3 us
    all_to_all x1, waiting for transfers between devices, on_device(): lax.all_to_all(split_heads(value_tangent), 'seq', split_axis=1, concat_ax...  15.4 us
  transfers between devices with their start and end apart: 9, of which 8 were waited for; matrix products, arithmetic and copies ran while one was open for 9% of the time, Pallas kernels for 0%

commit v1 on v0

v1 whole, which is shorter than its diff:
```python
import functools
import math

import jax
import jax.numpy as jnp
from jax import lax
from jax.experimental import pallas as pl
from jax.experimental.pallas import tpu as pltpu
from jax.sharding import PartitionSpec as P

HDIM = 128
BLOCK = 256
MASKED = -1e30


def pack_kernel(*refs):
    out_ref = refs[-1]
    for place, ref in enumerate(refs[:-1]):
        out_ref[0, place] = ref[0]


def pack_head(arrays, head, heads_here):
    _, tokens, width = arrays[0].shape
    groups = width // (heads_here * HDIM)
    count = len(arrays)
    return pl.pallas_call(
        pack_kernel,
        grid=(groups,),
        in_specs=[
            pl.BlockSpec((1, tokens, HDIM), lambda g: (0, 0, g * heads_here + head))
        ]
        * count,
        out_specs=pl.BlockSpec((1, count, tokens, HDIM), lambda g: (g, 0, 0, 0)),
        out_shape=jax.ShapeDtypeStruct((groups, count, tokens, HDIM), jnp.bfloat16),
        cost_estimate=pl.CostEstimate(
            flops=0, bytes_accessed=4 * count * groups * tokens * HDIM, transcendentals=0
        ),
    )(*arrays)


def unpack_kernel(*refs):
    heads = len(refs) - 2
    for head in range(heads):
        for place in range(2):
            refs[heads + place][0, :, head * HDIM : (head + 1) * HDIM] = refs[head][0, place]


def unpack(parts):
    groups, _, tokens, _ = parts[0].shape
    heads = len(parts)
    out = jax.ShapeDtypeStruct((1, tokens, groups * heads * HDIM), jnp.bfloat16)
    out_spec = pl.BlockSpec((1, tokens, heads * HDIM), lambda g: (0, 0, g))
    return pl.pallas_call(
        unpack_kernel,
        grid=(groups,),
        in_specs=[pl.BlockSpec((1, 2, tokens, HDIM), lambda g: (g, 0, 0, 0))] * heads,
        out_specs=[out_spec, out_spec],
        out_shape=[out, out],
        cost_estimate=pl.CostEstimate(
            flops=0, bytes_accessed=8 * heads * groups * tokens * HDIM, transcendentals=0
        ),
    )(*parts)


def attention_kernel(len_ref, in_ref, gate_ref, out_ref, kx, kk, vv, vo, scores, row_peak):
    groups, _, tokens, _ = in_ref.shape
    length = groups * tokens
    first_len = len_ref[0, 0]
    scale = 1.0 / math.sqrt(HDIM)
    exp2_scale = scale * math.log2(math.e)
    lane = lax.broadcasted_iota(jnp.int32, (tokens, HDIM), 1)
    ones = jnp.ones((tokens, HDIM), jnp.bfloat16)

    def fill(g, carry):
        rows = pl.ds(pl.multiple_of(g * tokens, tokens), tokens)
        key = in_ref[g, 1]
        value = in_ref[g, 2]
        place = g * tokens + lax.broadcasted_iota(jnp.int32, (tokens, HDIM), 0)
        other = jnp.where(place >= first_len, 0, 1)
        key_side = jnp.where(lane == other, MASKED, 0.0).astype(jnp.bfloat16)
        key_side = jnp.where(lane < 2, key_side, jnp.zeros_like(key_side))
        kx[rows, :HDIM] = key
        kx[rows, HDIM:] = key_side
        kk[rows, :HDIM] = key
        kk[rows, HDIM:] = in_ref[g, 4]
        vv[rows, :HDIM] = value
        vv[rows, HDIM:] = in_ref[g, 5]
        vo[rows, :HDIM] = value
        vo[rows, HDIM:] = ones
        return carry

    lax.fori_loop(0, groups, fill, 0)

    per = BLOCK // tokens
    nt = (((1,), (1,)), ((), ()))

    def one_block(block, carry):
        row0 = block * BLOCK
        query = in_ref[pl.ds(block * per, per), 0].reshape(BLOCK, HDIM)
        tangent = in_ref[pl.ds(block * per, per), 3].reshape(BLOCK, HDIM)
        place = row0 + lax.broadcasted_iota(jnp.int32, (BLOCK, HDIM), 0)
        second = place >= first_len
        own = jnp.where(second, 1, 0)
        lanes = lax.broadcasted_iota(jnp.int32, (BLOCK, HDIM), 1)
        query_side = jnp.where(lanes == own, 1.0, 0.0).astype(jnp.bfloat16)
        left = jnp.concatenate([query, query_side], axis=1)
        left_tangent = jnp.concatenate([tangent, query], axis=1)
        low = jnp.where(row0 >= first_len, first_len // BLOCK, 0)
        high = jnp.where(
            row0 + BLOCK <= first_len, (first_len + BLOCK - 1) // BLOCK, length // BLOCK
        )

        row_peak[...] = jnp.full((BLOCK, HDIM), -jnp.inf, jnp.float32)

        def first_pass(step, inner):
            rows = pl.ds(pl.multiple_of(step * BLOCK, BLOCK), BLOCK)
            found = lax.dot_general(left, kx[rows, :], nt, preferred_element_type=jnp.float32)
            scores[step] = found
            peak = row_peak[...]
            for cut in range(BLOCK // HDIM):
                peak = jnp.maximum(peak, found[:, cut * HDIM : (cut + 1) * HDIM])
            row_peak[...] = peak
            return inner

        lax.fori_loop(low, high, first_pass, 0)
        peak = jnp.max(row_peak[...], axis=1, keepdims=True)

        def second_pass(step, inner):
            total, sum_v, sum_t = inner
            rows = pl.ds(pl.multiple_of(step * BLOCK, BLOCK), BLOCK)
            weights = jnp.exp2((scores[step] - peak) * exp2_scale)
            moved = lax.dot_general(
                left_tangent, kk[rows, :], nt, preferred_element_type=jnp.float32
            )
            for cut in range(BLOCK // HDIM):
                total = total + weights[:, cut * HDIM : (cut + 1) * HDIM]
            sum_v = sum_v + jnp.dot(
                weights.astype(jnp.bfloat16), vv[rows, :], preferred_element_type=jnp.float32
            )
            sum_t = sum_t + jnp.dot(
                (weights * moved).astype(jnp.bfloat16),
                vo[rows, :],
                preferred_element_type=jnp.float32,
            )
            return total, sum_v, sum_t

        total, sum_v, sum_t = lax.fori_loop(
            low,
            high,
            second_pass,
            (
                jnp.zeros((BLOCK, HDIM), jnp.float32),
                jnp.zeros((BLOCK, 2 * HDIM), jnp.float32),
                jnp.zeros((BLOCK, 2 * HDIM), jnp.float32),
            ),
        )
        inverse = 1.0 / jnp.sum(total, axis=1, keepdims=True)
        plain = sum_v[:, :HDIM] * inverse
        centre = sum_t[:, HDIM:] * inverse
        moved = scale * (sum_t[:, :HDIM] * inverse - centre * plain) + sum_v[:, HDIM:] * inverse
        plain = plain.astype(jnp.bfloat16).astype(jnp.float32)
        moved = moved.astype(jnp.bfloat16).astype(jnp.float32)
        gate = jnp.where(second, gate_ref[1:2, :], gate_ref[0:1, :])
        rate = jnp.where(second, gate_ref[3:4, :], gate_ref[2:3, :])
        attended = (gate * plain).astype(jnp.bfloat16)
        attended_tangent = (rate * plain + gate * moved).astype(jnp.bfloat16)
        target = pl.ds(block * per, per)
        out_ref[target, 0] = attended.reshape(per, tokens, HDIM)
        out_ref[target, 1] = attended_tangent.reshape(per, tokens, HDIM)
        return carry

    lax.fori_loop(0, length // BLOCK, one_block, 0)


def attend(lengths, packed, gates):
    groups, _, tokens, _ = packed.shape
    length = groups * tokens
    wide = pltpu.VMEM((length, 2 * HDIM), jnp.bfloat16)
    return pl.pallas_call(
        attention_kernel,
        in_specs=[
            pl.BlockSpec(memory_space=pltpu.SMEM),
            pl.BlockSpec(memory_space=pltpu.VMEM),
            pl.BlockSpec(memory_space=pltpu.VMEM),
        ],
        out_specs=pl.BlockSpec(memory_space=pltpu.VMEM),
        out_shape=jax.ShapeDtypeStruct((groups, 2, tokens, HDIM), jnp.bfloat16),
        scratch_shapes=[
            wide,
            wide,
            wide,
            wide,
            pltpu.VMEM((length // BLOCK, BLOCK, BLOCK), jnp.float32),
            pltpu.VMEM((BLOCK, HDIM), jnp.float32),
        ],
        compiler_params=pltpu.CompilerParams(vmem_limit_bytes=32 * 1024 * 1024),
        cost_estimate=pl.CostEstimate(
            flops=8 * length * length * HDIM,
            bytes_accessed=16 * length * HDIM,
            transcendentals=length * length,
        ),
    )(lengths, packed, gates)


def exchange(array):
    return lax.all_to_all(array, "seq", split_axis=0, concat_axis=0, tiled=True)


def pick_gates(gate_table, rate_table, timesteps, groups):
    steps_here, width = gate_table.shape
    here = width // groups
    column = lax.axis_index("seq") * here
    tables = jnp.concatenate(
        [
            lax.dynamic_slice_in_dim(gate_table, column, here, 1),
            lax.dynamic_slice_in_dim(rate_table, column, here, 1),
        ],
        axis=1,
    )
    wanted = timesteps.reshape(-1) - lax.axis_index("fsdp") * steps_here
    one_hot = (wanted[:, None] == jnp.arange(steps_here, dtype=jnp.int32)[None, :]).astype(
        jnp.float32
    )
    picks = jnp.dot(one_hot, tables, precision=lax.Precision.HIGHEST)
    picks = picks.reshape(timesteps.shape[0], timesteps.shape[1], 2 * here)
    mine = lax.psum_scatter(picks, "fsdp", scatter_dimension=0, tiled=True)
    mine = mine.reshape(2, 2, here // HDIM, HDIM)
    return mine.transpose(2, 1, 0, 3).reshape(here // HDIM, 4, HDIM)


def on_device(
    queries,
    key_states,
    value_states,
    query_tangent,
    key_tangent,
    value_tangent,
    gate_table,
    rate_table,
    timesteps,
    lengths,
):
    groups = lax.axis_size("seq")
    heads_here = queries.shape[2] // (groups * HDIM)
    arrays = (queries, key_states, value_states, query_tangent, key_tangent, value_tangent)
    gates = pick_gates(gate_table, rate_table, timesteps, groups)
    parts = []
    for head in range(heads_here):
        received = exchange(pack_head(arrays, head, heads_here))
        parts.append(exchange(attend(lengths, received, gates[head])))
    return tuple(unpack(parts))


def solution(mesh):
    rows = P("fsdp", "seq", None)
    table = P("fsdp", None)
    in_specs = (rows,) * 6 + (table, table, P(), table)
    return jax.shard_map(
        on_device, mesh=mesh, in_specs=in_specs, out_specs=(rows, rows), check_vma=False
    )
```

time: 530 us -> 376 us (0.71)
  Pallas kernels: 0 us -> 94.3 us
  waiting for transfers between devices: 283 us -> 200 us
  matrix products: 73.4 us -> 0.22 us
  local copies, waits for them, and re-layouts: 76 us -> 9.17 us
  starting transfers between devices: 58.9 us -> 21.1 us
  blocking collectives: 0 us -> 34.2 us
  other arithmetic: 18.4 us -> 0.01 us
    pallas_call x0 -> x5, Pallas kernels: none -> 94.3 us  [the longest x2 66.3 us: attend(): pl.pallas_call(attention_kernel, in_specs=[pl.BlockSpec(memory_space=pltp...]
    all_to_all x8 -> x3, waiting for transfers between devices: 137 us -> 63.3 us  [exchange(): return lax.all_to_all(array, 'seq', split_axis=0, concat_axis=0, tiled=True)]
    dot_general x50 -> x1, matrix products: 73.4 us -> 0.22 us  [pick_gates(): picks = jnp.dot(one_hot, tables, precision=lax.Precision.HIGHEST)]
    all_to_all x8 -> x3, starting transfers between devices: 58.9 us -> 21.1 us  [exchange(): return lax.all_to_all(array, 'seq', split_axis=0, concat_axis=0, tiled=True)]
    all_to_all x0 -> x1, blocking collectives: none -> 34.2 us  [exchange(): return lax.all_to_all(array, 'seq', split_axis=0, concat_axis=0, tiled=True)]
    reshape x8 -> x2, local copies, waits for them, and re-layouts: 13.9 us -> 0.69 us  [the longest x1 0.67 us: pick_gates(): picks = picks.reshape(timesteps.shape[0], timesteps.shape[1], 2 * here)]
    convert_element_type x15 -> x0, other arithmetic: 12.7 us -> none  [the longest x8 6.09 us: primal_block(): (exp_scores / jnp.sum(exp_scores, axis=1, keepdims=True)).astype(jnp.bflo...]
    convert_element_type x4 -> x0, local copies, waits for them, and re-layouts: 11.9 us -> none  [the longest x2 6.42 us: on_device(): plain_rows = back.reshape(tokens, feature_width).astype(jnp.float32)]
  transfers between devices with their start and end apart: 9 -> 4, of which waited for: 8 -> 2; matrix products, arithmetic and copies ran while one was open for 9% -> 1% of each run, Pallas kernels for 0% -> 20%
where the time goes in v1:
time: 376 us; the launch traced here: 373 us
  waiting for transfers between devices  200 us (53%)
  Pallas kernels  94.3 us (25%)
  blocking collectives  34.2 us (9%)
  starting transfers between devices  21.1 us (6%)
  between operations  14.2 us (4%)
  local copies, waits for them, and re-layouts  9.17 us (2%)
    unnamed x2, waiting for transfers between devices  137 us
    pallas_call x2, Pallas kernels, attend(): pl.pallas_call(attention_kernel, in_specs=[pl.BlockSpec(memory_space=pltp...  66.3 us
    all_to_all x3, waiting for transfers between devices, exchange(): return lax.all_to_all(array, 'seq', split_axis=0, concat_axis=0, tiled=True)  63.3 us
    all_to_all x1, blocking collectives, exchange(): return lax.all_to_all(array, 'seq', split_axis=0, concat_axis=0, tiled=True)  34.2 us
    all_to_all x3, starting transfers between devices, exchange(): return lax.all_to_all(array, 'seq', split_axis=0, concat_axis=0, tiled=True)  21.1 us
    pallas_call x2, Pallas kernels, pack_head(): pl.pallas_call(pack_kernel, grid=(groups,), in_specs=[pl.BlockSpec((1, to...  18.7 us
    pallas_call x1, Pallas kernels, unpack(): pl.pallas_call(unpack_kernel, grid=(groups,), in_specs=[pl.BlockSpec((1,...  9.33 us
  transfers between devices with their start and end apart: 4, of which 2 were waited for; matrix products, arithmetic and copies ran while one was open for 1% of the time, Pallas kernels for 20%

profile of v1, /device:TPU:5, one launch (start us, length us, event | category | flops | bytes accessed | tf_op | source)
XLA Modules:
  0.0 373.4 jit_solution(16267386831375567727)
XLA Ops:
  7.2 9.4 %shard_map.115 = bf16[16,6,128,128]{3,2,1,0:T(8,128)(2,1)} custom-call(bf16[1,128,4096]{2,1,0:T(8,128)(2,1)} %refs_0_.3, bf16[1,128,4096]{2,1,0:T(8,128)(2,1)} %refs_1_.3, bf16[1,128,4096]{2,1,0:T(8,128)(2,1)} %refs_2_.3, bf16[1,128,4096]{2,1,0:T(8,128)(2,1)} %refs_3_.3, bf16[1,128,4096]{2,1,0:T(8,128)(2,1)} %refs_4_.3, bf16[1,128,4096]{2,1,0:T(8,128)(2,1)} %refs_5_.3), custom_call_target="tpu_custom_call" | custom-call | bytes 6291456 | tf_op jit(solution)/shard_map/pallas_call | solution.py:26
  16.5 9.3 %all-to-all-start.2 = ((bf16[16,6,128,128]{3,2,1,0:T(8,128)(2,1)}), bf16[16,6,128,128]{3,2,1,0:T(8,128)(2,1)S(1)}, u32[]{:S(2)}, u32[]{:S(2)}) async-start(bf16[16,6,128,128]{3,2,1,0:T(8,128)(2,1)} %shard_map.115), calls=%async_computation.2 | async-start | bytes 6291456 | tf_op jit(solution)/shard_map/all_to_all | solution.py:206
  25.8 9.3 %shard_map.113 = bf16[16,6,128,128]{3,2,1,0:T(8,128)(2,1)} custom-call(bf16[1,128,4096]{2,1,0:T(8,128)(2,1)} %refs_0_.3, bf16[1,128,4096]{2,1,0:T(8,128)(2,1)} %refs_1_.3, bf16[1,128,4096]{2,1,0:T(8,128)(2,1)} %refs_2_.3, bf16[1,128,4096]{2,1,0:T(8,128)(2,1)} %refs_3_.3, bf16[1,128,4096]{2,1,0:T(8,128)(2,1)} %refs_4_.3, bf16[1,128,4096]{2,1,0:T(8,128)(2,1)} %refs_5_.3), custom_call_target="tpu_custom_call" | custom-call | bytes 6291456 | tf_op jit(solution)/shard_map/pallas_call | solution.py:26
  35.2 63.3 %all-to-all-done.2.in_ref = bf16[16,6,128,128]{3,2,1,0:T(8,128)(2,1)S(1)} async-done(((bf16[16,6,128,128]{3,2,1,0:T(8,128)(2,1)}), bf16[16,6,128,128]{3,2,1,0:T(8,128)(2,1)S(1)}, u32[]{:S(2)}, u32[]{:S(2)}) %all-to-all-start.2) | async-done | bytes 3145760 | tf_op jit(solution)/shard_map/all_to_all | solution.py:206
  98.5 1.7 copy-done
  100.1 4.0 %all-to-all-start = ((bf16[16,6,128,128]{3,2,1,0:T(8,128)(2,1)}), bf16[16,6,128,128]{3,2,1,0:T(8,128)(2,1)S(1)}, u32[]{:S(2)}, u32[]{:S(2)}) async-start(bf16[16,6,128,128]{3,2,1,0:T(8,128)(2,1)} %shard_map.113), calls=%async_computation | async-start | bytes 6291456 | tf_op jit(solution)/shard_map/all_to_all | solution.py:206
  104.1 0.0 all-reduce.3.cloned.1.call-start
  104.2 0.1 copy.16
  104.3 0.1 sub.15
  104.4 0.9 constant_dynamic-slice_fusion.1
  105.3 0.2 fusion
  105.5 0.7 reshape.23
  106.2 0.0 all-reduce.3.cloned.1.call-update
  106.2 0.6 dynamic-slice
  106.8 136.9 %all-reduce.3.cloned.1.call-done = f32[16,2,512]{2,1,0:T(2,128)} async-done(((f32[16,2,512]{2,1,0:T(2,128)}), f32[16,2,512]{2,1,0:T(2,128)}) %all-reduce.3.cloned.1.call-update) | async-done | bytes 65552
  243.7 1.3 constant_dynamic-slice_fusion
  245.1 1.9 copy-done.1
  246.9 33.2 %shard_map.116 = bf16[16,2,128,128]{3,2,1,0:T(8,128)(2,1)S(1)} custom-call(s32[1,2]{1,0:T(1,128)S(1)} %copy-done.4, bf16[16,6,128,128]{3,2,1,0:T(8,128)(2,1)S(1)} %copy-done.1, f32[4,128]{1,0:T(4,128)S(1)} %bitcast.4), custom_call_target="tpu_custom_call" | custom-call | flops 4294967296 | bytes 4194304 | tf_op jit(solution)/shard_map/pallas_call | solution.py:179
  280.1 1.0 copy-done.2
  281.1 7.8 %all-to-all-start.3 = ((bf16[16,2,128,128]{3,2,1,0:T(8,128)(2,1)}), bf16[16,2,128,128]{3,2,1,0:T(8,128)(2,1)}, u32[]{:S(2)}, u32[]{:S(2)}) async-start(bf16[16,2,128,128]{3,2,1,0:T(8,128)(2,1)} %copy-done.2), calls=%async_computation.3 | async-start | bytes 2097152 | tf_op jit(solution)/shard_map/all_to_all | solution.py:206
  288.9 33.2 %shard_map.114 = bf16[16,2,128,128]{3,2,1,0:T(8,128)(2,1)S(1)} custom-call(s32[1,2]{1,0:T(1,128)S(1)} %copy-done.4, bf16[16,6,128,128]{3,2,1,0:T(8,128)(2,1)S(1)} %all-to-all-done.in_ref, f32[4,128]{1,0:T(4,128)S(1)} %bitcast.5), custom_call_target="tpu_custom_call" | custom-call | flops 4294967296 | bytes 4194304 | tf_op jit(solution)/shard_map/pallas_call | solution.py:179
  322.1 1.0 copy-done.3
  323.0 34.2 %all_to_all.20.refs_0_ = bf16[16,2,128,128]{3,2,1,0:T(8,128)(2,1)} all-to-all(bf16[16,2,128,128]{3,2,1,0:T(8,128)(2,1)} %copy-done.3), channel_id=1, replica_groups=mesh['fsdp'=16,'seq'=16] {'seq'}, dimensions={0} | all-to-all | bytes 2097152 | tf_op jit(solution)/shard_map/all_to_all | solution.py:206
  357.2 9.3 %shard_map.117 = (bf16[1,128,4096]{2,1,0:T(8,128)(2,1)}, bf16[1,128,4096]{2,1,0:T(8,128)(2,1)}) custom-call(bf16[16,2,128,128]{3,2,1,0:T(8,128)(2,1)} %all_to_all.20.refs_0_, bf16[16,2,128,128]{3,2,1,0:T(8,128)(2,1)} %all-to-all-done.3.refs_1_), custom_call_target="tpu_custom_call" | custom-call | bytes 4194304 | tf_op jit(solution)/shard_map/pallas_call | solution.py:53
  (17 shorter events, 0.1 us)
Async XLA Ops:
  16.5 81.9 %all-to-all-start.2 = ((bf16[16,6,128,128]{3,2,1,0:T(8,128)(2,1)}), bf16[16,6,128,128]{3,2,1,0:T(8,128)(2,1)S(1)}, u32[]{:S(2)}, u32[]{:S(2)}) async-start(bf16[16,6,128,128]{3,2,1,0:T(8,128)(2,1)} %shard_map.115), calls=%async_computation.2 | async-start | bytes 6291456 | tf_op jit(solution)/shard_map/all_to_all | solution.py:206
  35.2 69.0 %copy-start.5 = (s32[16,2]{0,1:T(2,128)S(1)}, s32[16,2]{0,1:T(2,128)}, u32[]{:S(2)}) copy-start(s32[16,2]{0,1:T(2,128)} %param.18) | copy-start | bytes 388
  35.2 71.0 %copy-start.6 = (u32[256]{0:T(256)S(1)}, u32[256]{0:T(256)}, u32[]{:S(2)}) copy-start(u32[256]{0:T(256)} %constant.24) | copy-start | bytes 3076
  35.2 209.9 %copy-start.4 = (s32[1,2]{1,0:T(1,128)S(1)}, s32[1,2]{1,0:T(1,128)}, u32[]{:S(2)}) copy-start(s32[1,2]{1,0:T(1,128)} %len_ref.3) | copy-start | bytes 28
  98.5 1.7 copy-start
  100.1 180.9 %all-to-all-start = ((bf16[16,6,128,128]{3,2,1,0:T(8,128)(2,1)}), bf16[16,6,128,128]{3,2,1,0:T(8,128)(2,1)S(1)}, u32[]{:S(2)}, u32[]{:S(2)}) async-start(bf16[16,6,128,128]{3,2,1,0:T(8,128)(2,1)} %shard_map.113), calls=%async_computation | async-start | bytes 6291456 | tf_op jit(solution)/shard_map/all_to_all | solution.py:206
  104.1 139.6 %all-reduce.3.cloned.1.call-start = ((), (), s32[]{:S(2)}) async-start(), calls=%async_computation.4 | async-start | bytes 131072
  245.0 1.9 copy-start.1
  280.1 1.0 copy-start.2
  281.1 42.0 %all-to-all-start.3 = ((bf16[16,2,128,128]{3,2,1,0:T(8,128)(2,1)}), bf16[16,2,128,128]{3,2,1,0:T(8,128)(2,1)}, u32[]{:S(2)}, u32[]{:S(2)}) async-start(bf16[16,2,128,128]{3,2,1,0:T(8,128)(2,1)} %copy-done.2), calls=%async_computation.3 | async-start | bytes 2097152 | tf_op jit(solution)/shard_map/all_to_all | solution.py:206
  322.1 1.0 copy-start.3
Sparse Core Ops, SparseCore 0:
  108.2 135.4 all-reduce.2

commit v2 on v1

v2 whole, which is shorter than its diff:
```python
import functools
import math

import jax
import jax.numpy as jnp
from jax import lax
from jax.experimental import pallas as pl
from jax.experimental.pallas import tpu as pltpu
from jax.sharding import PartitionSpec as P

HDIM = 128
BLOCK = 256
GROUPS_A_STEP = 4
MASKED = -1e30


def pack_kernel(heads, *refs):
    arrays, parts = refs[:-heads], refs[-heads:]
    for place, ref in enumerate(arrays):
        for group in range(GROUPS_A_STEP):
            for head in range(heads):
                column = (group * heads + head) * HDIM
                parts[head][group, place] = ref[0, :, column : column + HDIM]


def pack(arrays, heads):
    _, tokens, width = arrays[0].shape
    groups = width // (heads * HDIM)
    count = len(arrays)
    part = jax.ShapeDtypeStruct((groups, count, tokens, HDIM), jnp.bfloat16)
    part_spec = pl.BlockSpec((GROUPS_A_STEP, count, tokens, HDIM), lambda g: (g, 0, 0, 0))
    row_spec = pl.BlockSpec((1, tokens, GROUPS_A_STEP * heads * HDIM), lambda g: (0, 0, g))
    return pl.pallas_call(
        functools.partial(pack_kernel, heads),
        grid=(groups // GROUPS_A_STEP,),
        in_specs=[row_spec] * count,
        out_specs=[part_spec] * heads,
        out_shape=[part] * heads,
        compiler_params=pltpu.CompilerParams(vmem_limit_bytes=32 * 1024 * 1024),
        cost_estimate=pl.CostEstimate(
            flops=0, bytes_accessed=4 * heads * count * groups * tokens * HDIM, transcendentals=0
        ),
    )(*arrays)


def unpack_kernel(*refs):
    heads = len(refs) - 2
    for head in range(heads):
        for group in range(GROUPS_A_STEP):
            column = (group * heads + head) * HDIM
            for place in range(2):
                refs[heads + place][0, :, column : column + HDIM] = refs[head][group, place]


def unpack(parts):
    groups, _, tokens, _ = parts[0].shape
    heads = len(parts)
    out = jax.ShapeDtypeStruct((1, tokens, groups * heads * HDIM), jnp.bfloat16)
    out_spec = pl.BlockSpec((1, tokens, GROUPS_A_STEP * heads * HDIM), lambda g: (0, 0, g))
    part_spec = pl.BlockSpec((GROUPS_A_STEP, 2, tokens, HDIM), lambda g: (g, 0, 0, 0))
    return pl.pallas_call(
        unpack_kernel,
        grid=(groups // GROUPS_A_STEP,),
        in_specs=[part_spec] * heads,
        out_specs=[out_spec, out_spec],
        out_shape=[out, out],
        compiler_params=pltpu.CompilerParams(vmem_limit_bytes=32 * 1024 * 1024),
        cost_estimate=pl.CostEstimate(
            flops=0, bytes_accessed=8 * heads * groups * tokens * HDIM, transcendentals=0
        ),
    )(*parts)


def attention_kernel(len_ref, in_ref, gate_ref, out_ref, kx, kk, vv, vo):
    groups, _, tokens, _ = in_ref.shape
    length = groups * tokens
    first_len = len_ref[0, 0]
    scale = 1.0 / math.sqrt(HDIM)
    exp2_scale = scale * math.log2(math.e)
    lane = lax.broadcasted_iota(jnp.int32, (tokens, HDIM), 1)
    ones = jnp.ones((tokens, HDIM), jnp.bfloat16)

    def fill(g, carry):
        rows = pl.ds(pl.multiple_of(g * tokens, tokens), tokens)
        key = in_ref[g, 1]
        value = in_ref[g, 2]
        place = g * tokens + lax.broadcasted_iota(jnp.int32, (tokens, HDIM), 0)
        other = jnp.where(place >= first_len, 0, 1)
        key_side = jnp.where(lane == other, MASKED, 0.0).astype(jnp.bfloat16)
        key_side = jnp.where(lane < 2, key_side, jnp.zeros_like(key_side))
        kx[rows, :HDIM] = key
        kx[rows, HDIM:] = key_side
        kk[rows, :HDIM] = key
        kk[rows, HDIM:] = in_ref[g, 4]
        vv[rows, :HDIM] = value
        vv[rows, HDIM:] = in_ref[g, 5]
        vo[rows, :HDIM] = value
        vo[rows, HDIM:] = ones
        return carry

    lax.fori_loop(0, groups, fill, 0)

    per = BLOCK // tokens
    nt = (((1,), (1,)), ((), ()))
    blocks = length // BLOCK

    def one_block(block, carry):
        row0 = block * BLOCK
        low = jnp.where(row0 >= first_len, first_len // BLOCK, 0)
        high = jnp.where(row0 + BLOCK <= first_len, (first_len + BLOCK - 1) // BLOCK, blocks)

        def with_width(width):
            query = in_ref[pl.ds(block * per, per), 0].reshape(BLOCK, HDIM)
            tangent = in_ref[pl.ds(block * per, per), 3].reshape(BLOCK, HDIM)
            place = row0 + lax.broadcasted_iota(jnp.int32, (BLOCK, HDIM), 0)
            second = place >= first_len
            own = jnp.where(second, 1, 0)
            lanes = lax.broadcasted_iota(jnp.int32, (BLOCK, HDIM), 1)
            query_side = jnp.where(lanes == own, 1.0, 0.0).astype(jnp.bfloat16)
            left = jnp.concatenate([query, query_side], axis=1)
            left_tangent = jnp.concatenate([tangent, query], axis=1)
            cuts = [
                pl.ds(pl.multiple_of((low + step) * BLOCK, BLOCK), BLOCK) for step in range(width)
            ]
            found = [
                lax.dot_general(left, kx[rows, :], nt, preferred_element_type=jnp.float32)
                for rows in cuts
            ]
            peak = functools.reduce(jnp.maximum, found)
            peak = jnp.max(peak, axis=1, keepdims=True)
            total = jnp.zeros((BLOCK, BLOCK), jnp.float32)
            plain_weights = []
            moved_weights = []
            for step, rows in enumerate(cuts):
                moved = lax.dot_general(
                    left_tangent, kk[rows, :], nt, preferred_element_type=jnp.float32
                )
                weights = jnp.exp2((found[step] - peak) * exp2_scale)
                total = total + weights
                plain_weights.append(weights.astype(jnp.bfloat16))
                moved_weights.append((weights * moved).astype(jnp.bfloat16))
            rows = pl.ds(pl.multiple_of(low * BLOCK, BLOCK), width * BLOCK)
            sum_v = jnp.dot(
                jnp.concatenate(plain_weights, axis=1),
                vv[rows, :],
                preferred_element_type=jnp.float32,
            )
            sum_t = jnp.dot(
                jnp.concatenate(moved_weights, axis=1),
                vo[rows, :],
                preferred_element_type=jnp.float32,
            )
            inverse = 1.0 / jnp.sum(total, axis=1, keepdims=True)
            plain = sum_v[:, :HDIM] * inverse
            centre = sum_t[:, HDIM:] * inverse
            moved = scale * (sum_t[:, :HDIM] * inverse - centre * plain)
            moved = moved + sum_v[:, HDIM:] * inverse
            plain = plain.astype(jnp.bfloat16).astype(jnp.float32)
            moved = moved.astype(jnp.bfloat16).astype(jnp.float32)
            gate = jnp.where(second, gate_ref[1:2, :], gate_ref[0:1, :])
            rate = jnp.where(second, gate_ref[3:4, :], gate_ref[2:3, :])
            attended = (gate * plain).astype(jnp.bfloat16)
            attended_tangent = (rate * plain + gate * moved).astype(jnp.bfloat16)
            target = pl.ds(block * per, per)
            out_ref[target, 0] = attended.reshape(per, tokens, HDIM)
            out_ref[target, 1] = attended_tangent.reshape(per, tokens, HDIM)

        for width in range(1, blocks + 1):
            pl.when(high - low == width)(functools.partial(with_width, width))
        return carry

    lax.fori_loop(0, blocks, one_block, 0)


def attend(lengths, packed, gates):
    groups, _, tokens, _ = packed.shape
    length = groups * tokens
    wide = pltpu.VMEM((length, 2 * HDIM), jnp.bfloat16)
    return pl.pallas_call(
        attention_kernel,
        in_specs=[
            pl.BlockSpec(memory_space=pltpu.SMEM),
            pl.BlockSpec(memory_space=pltpu.VMEM),
            pl.BlockSpec(memory_space=pltpu.VMEM),
        ],
        out_specs=pl.BlockSpec(memory_space=pltpu.VMEM),
        out_shape=jax.ShapeDtypeStruct((groups, 2, tokens, HDIM), jnp.bfloat16),
        scratch_shapes=[
            wide,
            wide,
            wide,
            wide,
        ],
        compiler_params=pltpu.CompilerParams(vmem_limit_bytes=32 * 1024 * 1024),
        cost_estimate=pl.CostEstimate(
            flops=8 * length * length * HDIM,
            bytes_accessed=16 * length * HDIM,
            transcendentals=length * length,
        ),
    )(lengths, packed, gates)


def exchange(array):
    return lax.all_to_all(array, "seq", split_axis=0, concat_axis=0, tiled=True)


def pick_gates(gate_table, rate_table, timesteps, groups):
    steps_here, width = gate_table.shape
    here = width // groups
    column = lax.axis_index("seq") * here
    tables = jnp.concatenate(
        [
            lax.dynamic_slice_in_dim(gate_table, column, here, 1),
            lax.dynamic_slice_in_dim(rate_table, column, here, 1),
        ],
        axis=1,
    )
    wanted = timesteps.reshape(-1) - lax.axis_index("fsdp") * steps_here
    one_hot = (wanted[:, None] == jnp.arange(steps_here, dtype=jnp.int32)[None, :]).astype(
        jnp.float32
    )
    picks = jnp.dot(one_hot, tables, precision=lax.Precision.HIGHEST)
    picks = picks.reshape(timesteps.shape[0], timesteps.shape[1], 2 * here)
    mine = lax.all_to_all(picks, "fsdp", split_axis=0, concat_axis=0, tiled=True).sum(axis=0)
    mine = mine.reshape(2, 2, here // HDIM, HDIM)
    return mine.transpose(2, 1, 0, 3).reshape(here // HDIM, 4, HDIM)


def on_device(
    queries,
    key_states,
    value_states,
    query_tangent,
    key_tangent,
    value_tangent,
    gate_table,
    rate_table,
    timesteps,
    lengths,
):
    groups = lax.axis_size("seq")
    heads_here = queries.shape[2] // (groups * HDIM)
    arrays = (queries, key_states, value_states, query_tangent, key_tangent, value_tangent)
    gates = pick_gates(gate_table, rate_table, timesteps, groups)
    parts = []
    for head, packed in enumerate(pack(arrays, heads_here)):
        parts.append(exchange(attend(lengths, exchange(packed), gates[head])))
    return tuple(unpack(parts))


def solution(mesh):
    rows = P("fsdp", "seq", None)
    table = P("fsdp", None)
    in_specs = (rows,) * 6 + (table, table, P(), table)
    return jax.shard_map(
        on_device, mesh=mesh, in_specs=in_specs, out_specs=(rows, rows), check_vma=False
    )
```

time: 376 us -> 249 us (0.66)
  waiting for transfers between devices: 200 us -> 71.7 us
  blocking collectives: 34.2 us -> 114 us
  Pallas kernels: 94.3 us -> 23.9 us
  between operations: 14.2 us -> 0.76 us
  local copies, waits for them, and re-layouts: 9.17 us -> 17.1 us
    unnamed x2 -> x0, waiting for transfers between devices: 137 us -> none
    all_to_all x1 -> x2, blocking collectives: 34.2 us -> 114 us  [exchange(): return lax.all_to_all(array, 'seq', split_axis=0, concat_axis=0, tiled=True)]
    pallas_call x2, Pallas kernels: 66.3 us -> 20.2 us  [attend(): pl.pallas_call(attention_kernel, in_specs=[pl.BlockSpec(memory_space=pltp...]
    pallas_call x3 -> x2, Pallas kernels: 28 us -> 3.65 us  [the longest x1 2.04 us: unpack(): pl.pallas_call(unpack_kernel, grid=(groups // GROUPS_A_STEP,), in_specs=[...]
    all_to_all x3 -> x2, starting transfers between devices: 21.1 us -> 9.81 us  [exchange(): return lax.all_to_all(array, 'seq', split_axis=0, concat_axis=0, tiled=True)]
    all_to_all x3 -> x2, waiting for transfers between devices: 63.3 us -> 71.7 us  [exchange(): return lax.all_to_all(array, 'seq', split_axis=0, concat_axis=0, tiled=True)]
    unnamed x16 -> x24, local copies, waits for them, and re-layouts: 7.41 us -> 15.4 us
    all_to_all x0 -> x1, starting transfers between devices: none -> 7.76 us  [pick_gates(): lax.all_to_all(picks, 'fsdp', split_axis=0, concat_axis=0, tiled=True)]
  transfers between devices with their start and end apart: 4 -> 3, of which waited for: 2 -> 2; matrix products, arithmetic and copies ran while one was open for 1% -> 0% of each run, Pallas kernels for 20% -> 9%
where the time goes in v2:
time: 249 us; the launch traced here: 246 us
  blocking collectives  114 us (46%)
  waiting for transfers between devices  71.7 us (29%)
  Pallas kernels  23.9 us (10%)
  starting transfers between devices  17.6 us (7%)
  local copies, waits for them, and re-layouts  17.1 us (7%)
    all_to_all x2, blocking collectives, exchange(): return lax.all_to_all(array, 'seq', split_axis=0, concat_axis=0, tiled=True)  114 us
    all_to_all x2, waiting for transfers between devices, exchange(): return lax.all_to_all(array, 'seq', split_axis=0, concat_axis=0, tiled=True)  71.7 us
    pallas_call x2, Pallas kernels, attend(): pl.pallas_call(attention_kernel, in_specs=[pl.BlockSpec(memory_space=pltp...  20.2 us
    unnamed x24, local copies, waits for them, and re-layouts  15.4 us
    all_to_all x2, starting transfers between devices, exchange(): return lax.all_to_all(array, 'seq', split_axis=0, concat_axis=0, tiled=True)  9.81 us
    all_to_all x1, starting transfers between devices, pick_gates(): lax.all_to_all(picks, 'fsdp', split_axis=0, concat_axis=0, tiled=True)  7.76 us
  transfers between devices with their start and end apart: 3, of which 2 were waited for; matrix products, arithmetic and copies ran while one was open for 0% of the time, Pallas kernels for 9%

profile of v2, /device:TPU:5, one launch (start us, length us, event | category | flops | bytes accessed | tf_op | source)
XLA Modules:
  0.0 245.7 jit_solution(6909126249738548414)
XLA Ops:
  0.6 0.7 broadcast_subtract_fusion
  1.5 0.9 constant_dynamic-slice_fusion
  3.3 7.8 %all-to-all-start.1 = ((f32[16,2,512]{2,1,0:T(2,128)}), f32[16,2,512]{2,1,0:T(2,128)S(1)}, u32[]{:S(2)}, u32[]{:S(2)}) async-start(f32[16,2,512]{2,1,0:T(2,128)} %reshape.23), calls=%async_computation.1 | async-start | bytes 131072 | tf_op jit(solution)/shard_map/all_to_all | solution.py:224
  11.1 1.2 copy-done.5
  12.3 1.2 copy-done.6
  13.5 1.2 copy-done.7
  14.7 1.2 copy-done.8
  15.9 1.2 copy-done.9
  17.2 1.2 copy-done.10
  18.4 1.6 shard_map.113
  20.0 1.6 copy-done.2
  21.7 80.5 %all_to_all.25.in_ref = bf16[16,6,128,128]{3,2,1,0:T(8,128)(2,1)} all-to-all(bf16[16,6,128,128]{3,2,1,0:T(8,128)(2,1)S(1)} %get-tuple-element.4), channel_id=1, replica_groups=mesh['fsdp'=16,'seq'=16] {'seq'}, dimensions={0} | all-to-all | bytes 6291456 | tf_op jit(solution)/shard_map/all_to_all | solution.py:204
  102.2 4.5 %all-to-all-start.3 = ((bf16[16,6,128,128]{3,2,1,0:T(8,128)(2,1)}), bf16[16,6,128,128]{3,2,1,0:T(8,128)(2,1)S(1)}, u32[]{:S(2)}, u32[]{:S(2)}) async-start(bf16[16,6,128,128]{3,2,1,0:T(8,128)(2,1)} %copy-done.2), calls=%async_computation.3 | async-start | bytes 6291456 | tf_op jit(solution)/shard_map/all_to_all | solution.py:204
  106.8 1.9 copy-done.3
  108.7 10.1 %shard_map.114 = bf16[16,2,128,128]{3,2,1,0:T(8,128)(2,1)S(1)} custom-call(s32[1,2]{1,0:T(1,128)S(1)} %copy-done.11, bf16[16,6,128,128]{3,2,1,0:T(8,128)(2,1)S(1)} %copy-done.3, f32[4,128]{1,0:T(4,128)S(1)} %bitcast.3), custom_call_target="tpu_custom_call" | custom-call | flops 4294967296 | bytes 4194304 | tf_op jit(solution)/shard_map/pallas_call | solution.py:179
  118.8 1.0 copy-done.4
  119.8 58.5 %all-to-all-done.3.in_ref = bf16[16,6,128,128]{3,2,1,0:T(8,128)(2,1)S(1)} async-done(((bf16[16,6,128,128]{3,2,1,0:T(8,128)(2,1)}), bf16[16,6,128,128]{3,2,1,0:T(8,128)(2,1)S(1)}, u32[]{:S(2)}, u32[]{:S(2)}) %all-to-all-start.3) | async-done | bytes 3145760 | tf_op jit(solution)/shard_map/all_to_all | solution.py:204
  178.3 1.6 copy-done
  179.9 5.3 %all-to-all-start.2 = ((bf16[16,2,128,128]{3,2,1,0:T(8,128)(2,1)}), bf16[16,2,128,128]{3,2,1,0:T(8,128)(2,1)S(1)}, u32[]{:S(2)}, u32[]{:S(2)}) async-start(bf16[16,2,128,128]{3,2,1,0:T(8,128)(2,1)} %copy-done.4), calls=%async_computation.2 | async-start | bytes 2097152 | tf_op jit(solution)/shard_map/all_to_all | solution.py:204
  185.2 1.9 copy-done.1
  187.1 10.1 %shard_map.115 = bf16[16,2,128,128]{3,2,1,0:T(8,128)(2,1)S(1)} custom-call(s32[1,2]{1,0:T(1,128)S(1)} %copy-done.11, bf16[16,6,128,128]{3,2,1,0:T(8,128)(2,1)S(1)} %copy-done.1, f32[4,128]{1,0:T(4,128)S(1)} %bitcast.4), custom_call_target="tpu_custom_call" | custom-call | flops 4294967296 | bytes 4194304 | tf_op jit(solution)/shard_map/pallas_call | solution.py:179
  197.2 13.2 %all-to-all-done.2.refs_0_ = bf16[16,2,128,128]{3,2,1,0:T(8,128)(2,1)S(1)} async-done(((bf16[16,2,128,128]{3,2,1,0:T(8,128)(2,1)}), bf16[16,2,128,128]{3,2,1,0:T(8,128)(2,1)S(1)}, u32[]{:S(2)}, u32[]{:S(2)}) %all-to-all-start.2) | async-done | bytes 1048608 | tf_op jit(solution)/shard_map/all_to_all | solution.py:204
  210.4 33.3 %all_to_all.26.refs_1_ = bf16[16,2,128,128]{3,2,1,0:T(8,128)(2,1)S(1)} all-to-all(bf16[16,2,128,128]{3,2,1,0:T(8,128)(2,1)S(1)} %shard_map.115), channel_id=1, replica_groups=mesh['fsdp'=16,'seq'=16] {'seq'}, dimensions={0} | all-to-all | bytes 2097152 | tf_op jit(solution)/shard_map/all_to_all | solution.py:204
  243.7 2.0 shard_map.116
  (23 shorter events, 1.2 us)
Async XLA Ops:
  3.3 18.4 %all-to-all-start.1 = ((f32[16,2,512]{2,1,0:T(2,128)}), f32[16,2,512]{2,1,0:T(2,128)S(1)}, u32[]{:S(2)}, u32[]{:S(2)}) async-start(f32[16,2,512]{2,1,0:T(2,128)} %reshape.23), calls=%async_computation.1 | async-start | bytes 131072 | tf_op jit(solution)/shard_map/all_to_all | solution.py:224
  11.0 1.2 copy-start.5
  12.3 1.2 copy-start.6
  13.5 1.2 copy-start.7
  14.7 1.2 copy-start.8
  15.9 1.2 copy-start.9
  17.2 1.2 copy-start.10
  20.0 1.6 copy-start.2
  102.2 4.6 %copy-start.11 = (s32[1,2]{1,0:T(1,128)S(1)}, s32[1,2]{1,0:T(1,128)}, u32[]{:S(2)}) copy-start(s32[1,2]{1,0:T(1,128)} %len_ref.3) | copy-start | bytes 28
  102.2 76.1 %all-to-all-start.3 = ((bf16[16,6,128,128]{3,2,1,0:T(8,128)(2,1)}), bf16[16,6,128,128]{3,2,1,0:T(8,128)(2,1)S(1)}, u32[]{:S(2)}, u32[]{:S(2)}) async-start(bf16[16,6,128,128]{3,2,1,0:T(8,128)(2,1)} %copy-done.2), calls=%async_computation.3 | async-start | bytes 6291456 | tf_op jit(solution)/shard_map/all_to_all | solution.py:204
  106.8 1.9 copy-start.3
  118.8 1.0 copy-start.4
  178.3 1.6 copy-start
  179.9 30.5 %all-to-all-start.2 = ((bf16[16,2,128,128]{3,2,1,0:T(8,128)(2,1)}), bf16[16,2,128,128]{3,2,1,0:T(8,128)(2,1)S(1)}, u32[]{:S(2)}, u32[]{:S(2)}) async-start(bf16[16,2,128,128]{3,2,1,0:T(8,128)(2,1)} %copy-done.4), calls=%async_computation.2 | async-start | bytes 2097152 | tf_op jit(solution)/shard_map/all_to_all | solution.py:204
  185.2 1.9 copy-start.1

commit v3 on v2

v3 whole, which is shorter than its diff:
```python
import functools
import math

import jax
import jax.numpy as jnp
from jax import lax
from jax.experimental import pallas as pl
from jax.experimental.pallas import tpu as pltpu
from jax.sharding import PartitionSpec as P

HDIM = 128
BLOCK = 256
GROUPS_A_STEP = 4
ARRAYS = 6
MASKED = -1e30
WIDTHS = (2, 3, 4, 5, 6)
MIB = 1024 * 1024


def pack_kernel(heads, *refs):
    arrays, parts = refs[:-heads], refs[-heads:]
    for place, ref in enumerate(arrays):
        for group in range(GROUPS_A_STEP):
            for head in range(heads):
                column = (group * heads + head) * HDIM
                parts[head][group, place] = ref[0, :, column : column + HDIM]


def pack(arrays, heads):
    _, tokens, width = arrays[0].shape
    groups = width // (heads * HDIM)
    part = (ARRAYS, tokens, HDIM)
    row_spec = pl.BlockSpec((1, tokens, GROUPS_A_STEP * heads * HDIM), lambda g: (0, 0, g))
    part_spec = pl.BlockSpec((GROUPS_A_STEP,) + part, lambda g: (g, 0, 0, 0))
    return pl.pallas_call(
        functools.partial(pack_kernel, heads),
        grid=(groups // GROUPS_A_STEP,),
        in_specs=[row_spec] * ARRAYS,
        out_specs=[part_spec] * heads,
        out_shape=[jax.ShapeDtypeStruct((groups,) + part, jnp.bfloat16)] * heads,
        compiler_params=pltpu.CompilerParams(vmem_limit_bytes=56 * MIB),
        cost_estimate=pl.CostEstimate(
            flops=0, bytes_accessed=4 * ARRAYS * tokens * width, transcendentals=0
        ),
    )(*arrays)


def unpack_kernel(*refs):
    heads = len(refs) - 2
    for head in range(heads):
        for group in range(GROUPS_A_STEP):
            column = (group * heads + head) * HDIM
            for place in range(2):
                refs[heads + place][0, :, column : column + HDIM] = refs[head][group, place]


def unpack(parts):
    groups, _, tokens, _ = parts[0].shape
    heads = len(parts)
    out = jax.ShapeDtypeStruct((1, tokens, groups * heads * HDIM), jnp.bfloat16)
    out_spec = pl.BlockSpec((1, tokens, GROUPS_A_STEP * heads * HDIM), lambda g: (0, 0, g))
    part_spec = pl.BlockSpec((GROUPS_A_STEP, 2, tokens, HDIM), lambda g: (g, 0, 0, 0))
    return pl.pallas_call(
        unpack_kernel,
        grid=(groups // GROUPS_A_STEP,),
        in_specs=[part_spec] * heads,
        out_specs=[out_spec, out_spec],
        out_shape=[out, out],
        compiler_params=pltpu.CompilerParams(vmem_limit_bytes=32 * MIB),
        cost_estimate=pl.CostEstimate(
            flops=0, bytes_accessed=8 * heads * groups * tokens * HDIM, transcendentals=0
        ),
    )(*parts)


def attention_kernel(len_ref, in_ref, gate_ref, query_side, key_side, out_ref):
    groups, _, tokens, _ = in_ref.shape
    length = groups * tokens
    first_len = len_ref[0, 0]
    scale = 1.0 / math.sqrt(HDIM)
    exp2_scale = scale * math.log2(math.e)
    nt = (((1,), (1,)), ((), ()))
    per = BLOCK // tokens
    blocks = length // BLOCK
    row = lax.broadcasted_iota(jnp.int32, (BLOCK, HDIM), 0)

    def rows_of(block, count, place):
        found = in_ref[pl.ds(block * per, count * per), place]
        return found.reshape(count * BLOCK, HDIM)

    def beside(*pieces):
        return jnp.concatenate(pieces, axis=1)

    def one_block(block, carry):
        row0 = pl.multiple_of(block * BLOCK, BLOCK)
        second = row0 + row >= first_len
        low = jnp.where(row0 >= first_len, first_len // BLOCK, 0)
        high = jnp.where(row0 + BLOCK <= first_len, (first_len + BLOCK - 1) // BLOCK, blocks)

        def score(low, width):
            left = beside(rows_of(block, 1, 0), query_side[pl.ds(row0, BLOCK), :])
            found = []
            for step in range(width):
                start = pl.multiple_of((low + step) * BLOCK, BLOCK)
                right = beside(rows_of(low + step, 1, 1), key_side[pl.ds(start, BLOCK), :])
                found.append(
                    lax.dot_general(left, right, nt, preferred_element_type=jnp.float32)
                )
            halves = [f[:, i : i + HDIM] for f in found for i in range(0, BLOCK, HDIM)]
            peak = jnp.max(functools.reduce(jnp.maximum, halves), axis=1, keepdims=True)
            return found, peak

        def weigh(low, found, peak):
            left = beside(rows_of(block, 1, 3), rows_of(block, 1, 0))
            total = jnp.zeros((BLOCK, HDIM), jnp.float32)
            plain_weights = []
            moved_weights = []
            for step, scores in enumerate(found):
                right = beside(rows_of(low + step, 1, 1), rows_of(low + step, 1, 4))
                moved = lax.dot_general(left, right, nt, preferred_element_type=jnp.float32)
                weights = jnp.exp2((scores - peak) * exp2_scale)
                for i in range(0, BLOCK, HDIM):
                    total = total + weights[:, i : i + HDIM]
                plain_weights.append(weights.astype(jnp.bfloat16))
                moved_weights.append((weights * moved).astype(jnp.bfloat16))
            return total, beside(*plain_weights), beside(*moved_weights)

        def combine(low, width, plain_weights, moved_weights):
            value = rows_of(low, width, 2)
            sum_v = jnp.dot(
                plain_weights,
                beside(value, rows_of(low, width, 5)),
                preferred_element_type=jnp.float32,
            )
            sum_t = jnp.dot(
                moved_weights,
                beside(value, jnp.ones((width * BLOCK, HDIM), jnp.bfloat16)),
                preferred_element_type=jnp.float32,
            )
            return sum_v, sum_t

        def finish(total, sum_v, sum_t):
            inverse = 1.0 / jnp.sum(total, axis=1, keepdims=True)
            plain = sum_v[:, :HDIM] * inverse
            centre = sum_t[:, HDIM:] * inverse
            moved = scale * (sum_t[:, :HDIM] * inverse - centre * plain)
            moved = moved + sum_v[:, HDIM:] * inverse
            plain = plain.astype(jnp.bfloat16).astype(jnp.float32)
            moved = moved.astype(jnp.bfloat16).astype(jnp.float32)
            gate = jnp.where(second, gate_ref[1:2, :], gate_ref[0:1, :])
            rate = jnp.where(second, gate_ref[3:4, :], gate_ref[2:3, :])
            attended = (gate * plain).astype(jnp.bfloat16)
            attended_tangent = (rate * plain + gate * moved).astype(jnp.bfloat16)
            target = pl.ds(block * per, per)
            out_ref[target, 0] = attended.reshape(per, tokens, HDIM)
            out_ref[target, 1] = attended_tangent.reshape(per, tokens, HDIM)

        def with_width(width):
            first = jnp.minimum(low, blocks - width)
            found, peak = score(first, width)
            total, plain_weights, moved_weights = weigh(first, found, peak)
            finish(total, *combine(first, width, plain_weights, moved_weights))

        widths = [width for width in WIDTHS if width < blocks] + [blocks]
        for below, width in zip([0] + widths, widths):
            fits = (high - low > below) & (high - low <= width)
            pl.when(fits)(functools.partial(with_width, width))
        return carry

    lax.fori_loop(0, blocks, one_block, 0)


def sides(first_len, length):
    own = (jnp.arange(length, dtype=jnp.int32) >= first_len).astype(jnp.int32)[:, None]
    lane = jnp.arange(HDIM, dtype=jnp.int32)[None, :]
    query_side = jnp.where(lane == own, 1.0, 0.0).astype(jnp.bfloat16)
    key_side = jnp.where(lane == 1 - own, MASKED, 0.0).astype(jnp.bfloat16)
    return query_side, key_side


def attend(lengths, received, gates, query_side, key_side):
    groups, _, tokens, _ = received.shape
    length = groups * tokens
    in_vmem = pl.BlockSpec(memory_space=pltpu.VMEM)
    return pl.pallas_call(
        attention_kernel,
        in_specs=[pl.BlockSpec(memory_space=pltpu.SMEM)] + [in_vmem] * 4,
        out_specs=in_vmem,
        out_shape=jax.ShapeDtypeStruct((groups, 2, tokens, HDIM), jnp.bfloat16),
        compiler_params=pltpu.CompilerParams(vmem_limit_bytes=32 * MIB),
        cost_estimate=pl.CostEstimate(
            flops=8 * length * length * HDIM,
            bytes_accessed=16 * length * HDIM,
            transcendentals=length * length,
        ),
    )(lengths, received, gates, query_side, key_side)


def exchange(array):
    return lax.all_to_all(array, "seq", split_axis=0, concat_axis=0, tiled=True)


def pick_gates(gate_table, rate_table, timesteps, groups):
    steps_here, width = gate_table.shape
    here = width // groups
    column = lax.axis_index("seq") * here
    tables = jnp.concatenate(
        [
            lax.dynamic_slice_in_dim(gate_table, column, here, 1),
            lax.dynamic_slice_in_dim(rate_table, column, here, 1),
        ],
        axis=1,
    )
    me = lax.axis_index("fsdp")
    wanted = timesteps.reshape(-1) - me * steps_here
    one_hot = (wanted[:, None] == jnp.arange(steps_here, dtype=jnp.int32)[None, :]).astype(
        jnp.float32
    )
    picks = jnp.dot(one_hot, tables, precision=lax.Precision.HIGHEST)
    size = lax.axis_size("fsdp")
    picks = picks.reshape(size, -1)
    bit = size // 2
    while bit:
        mine = (me // bit) % 2
        halves = picks.reshape(2, bit, -1)
        kept = lax.dynamic_index_in_dim(halves, mine, 0, keepdims=False)
        sent = lax.dynamic_index_in_dim(halves, 1 - mine, 0, keepdims=False)
        picks = kept + lax.ppermute(sent, "fsdp", [(i, i ^ bit) for i in range(size)])
        bit //= 2
    mine = picks.reshape(2, 2, here // HDIM, HDIM)
    return mine.transpose(2, 1, 0, 3).reshape(here // HDIM, 4, HDIM)


def on_device(
    queries,
    key_states,
    value_states,
    query_tangent,
    key_tangent,
    value_tangent,
    gate_table,
    rate_table,
    timesteps,
    lengths,
):
    groups = lax.axis_size("seq")
    heads = queries.shape[2] // (groups * HDIM)
    arrays = (queries, key_states, value_states, query_tangent, key_tangent, value_tangent)
    packed = pack(arrays, heads)
    gates = pick_gates(gate_table, rate_table, timesteps, groups)
    query_side, key_side = sides(lengths[0, 0], groups * queries.shape[1])
    parts = []
    for head in range(heads):
        received = exchange(packed[head])
        parts.append(attend(lengths, received, gates[head], query_side, key_side))
    return tuple(unpack([exchange(part) for part in parts]))


def solution(mesh):
    rows = P("fsdp", "seq", None)
    table = P("fsdp", None)
    in_specs = (rows,) * 6 + (table, table, P(), table)
    return jax.shard_map(
        on_device, mesh=mesh, in_specs=in_specs, out_specs=(rows, rows), check_vma=False
    )
```

time: 249 us -> 234 us (0.940)
  waiting for transfers between devices: 71.7 us -> 54.5 us
  Pallas kernels: 23.9 us -> 29.2 us
  local copies, waits for them, and re-layouts: 17.1 us -> 12.7 us
    all_to_all x2, waiting for transfers between devices: 71.7 us -> 45.5 us  [exchange(): return lax.all_to_all(array, 'seq', split_axis=0, concat_axis=0, tiled=True)]
    ppermute x0 -> x4, waiting for transfers between devices: none -> 9 us  [pick_gates(): lax.ppermute(sent, 'fsdp', [(i, i ^ bit) for i in range(size)])]
    ppermute x0 -> x4, starting transfers between devices: none -> 7.91 us  [pick_gates(): lax.ppermute(sent, 'fsdp', [(i, i ^ bit) for i in range(size)])]
    all_to_all x1 -> x0, starting transfers between devices: 7.76 us -> none  [pick_gates(): lax.all_to_all(picks, 'fsdp', split_axis=0, concat_axis=0, tiled=True)]
    pallas_call x1, Pallas kernels: 1.61 us -> 6.12 us  [pack(): pl.pallas_call(functools.partial(pack_kernel, heads), grid=(groups // GRO...]
    unnamed x24 -> x22, local copies, waits for them, and re-layouts: 15.4 us -> 11.5 us
  transfers between devices with their start and end apart: 3 -> 6, of which waited for: 2 -> 5; matrix products, arithmetic and copies ran while one was open for 0% -> 2% of each run, Pallas kernels for 9% -> 9%
where the time goes in v3:
time: 234 us; the launch traced here: 232 us
  blocking collectives  115 us (49%)
  waiting for transfers between devices  54.5 us (23%)
  Pallas kernels  29.2 us (12%)
  starting transfers between devices  17.4 us (7%)
  local copies, waits for them, and re-layouts  12.7 us (5%)
    all_to_all x2, blocking collectives, exchange(): return lax.all_to_all(array, 'seq', split_axis=0, concat_axis=0, tiled=True)  115 us
    all_to_all x2, waiting for transfers between devices, exchange(): return lax.all_to_all(array, 'seq', split_axis=0, concat_axis=0, tiled=True)  45.5 us
    pallas_call x2, Pallas kernels, attend(): pl.pallas_call(attention_kernel, in_specs=[pl.BlockSpec(memory_space=pltp...  21 us
    unnamed x22, local copies, waits for them, and re-layouts  11.5 us
    all_to_all x2, starting transfers between devices, exchange(): return lax.all_to_all(array, 'seq', split_axis=0, concat_axis=0, tiled=True)  9.54 us
    ppermute x4, waiting for transfers between devices, pick_gates(): lax.ppermute(sent, 'fsdp', [(i, i ^ bit) for i in range(size)])  9 us
    ppermute x4, starting transfers between devices, pick_gates(): lax.ppermute(sent, 'fsdp', [(i, i ^ bit) for i in range(size)])  7.91 us
    pallas_call x1, Pallas kernels, pack(): pl.pallas_call(functools.partial(pack_kernel, heads), grid=(groups // GRO...  6.12 us
  transfers between devices with their start and end apart: 6, of which 5 were waited for; matrix products, arithmetic and copies ran while one was open for 2% of the time, Pallas kernels for 9%

profile of v3, /device:TPU:5, one launch (start us, length us, event | category | flops | bytes accessed | tf_op | source)
XLA Modules:
  0.0 231.9 jit_solution(14565276719038378322)
XLA Ops:
  0.6 6.1 %shard_map.113 = (bf16[16,6,128,128]{3,2,1,0:T(8,128)(2,1)}, bf16[16,6,128,128]{3,2,1,0:T(8,128)(2,1)}) custom-call(bf16[1,128,4096]{2,1,0:T(8,128)(2,1)} %refs_0_.1, bf16[1,128,4096]{2,1,0:T(8,128)(2,1)} %refs_1_.1, bf16[1,128,4096]{2,1,0:T(8,128)(2,1)} %refs_2_.1, bf16[1,128,4096]{2,1,0:T(8,128)(2,1)} %refs_3_.1, bf16[1,128,4096]{2,1,0:T(8,128)(2,1)} %refs_4_.1, ...), custom_call_target="tpu_custom_call" | custom-call | bytes 12582912 | tf_op jit(solution)/shard_map/pallas_call | solution.py:35
  6.8 81.2 %all_to_all.20.in_ref = bf16[16,6,128,128]{3,2,1,0:T(8,128)(2,1)} all-to-all(bf16[16,6,128,128]{3,2,1,0:T(8,128)(2,1)} %get-tuple-element.4), channel_id=1, replica_groups=mesh['fsdp'=16,'seq'=16] {'seq'}, dimensions={0} | all-to-all | bytes 6291456 | tf_op jit(solution)/shard_map/all_to_all | solution.py:200
  87.9 4.9 %all-to-all-start.2 = ((bf16[16,6,128,128]{3,2,1,0:T(8,128)(2,1)}), bf16[16,6,128,128]{3,2,1,0:T(8,128)(2,1)S(1)}, u32[]{:S(2)}, u32[]{:S(2)}) async-start(bf16[16,6,128,128]{3,2,1,0:T(8,128)(2,1)} %get-tuple-element.5), calls=%async_computation.2 | async-start | bytes 6291456 | tf_op jit(solution)/shard_map/all_to_all | solution.py:200
  94.3 2.7 %collective-permute-start = (f32[8,1024]{1,0:T(8,128)S(1)}, f32[8,1024]{1,0:T(8,128)S(1)}, u32[]{:S(2)}, u32[]{:S(2)}) collective-permute-start(f32[8,1024]{1,0:T(8,128)S(1)} %dynamic-slice_bitcast_fusion), channel_id=1, source_target_pairs={{0,128},{16,144},{32,160},{48,176},{64,192},{80,208},{96,224},{112... | collective-permute-start | bytes 98312 | tf_op jit(solution)/shard_map/ppermute | solution.py:228
  97.0 3.1 %collective-permute-done = f32[8,1024]{1,0:T(8,128)S(1)} collective-permute-done((f32[8,1024]{1,0:T(8,128)S(1)}, f32[8,1024]{1,0:T(8,128)S(1)}, u32[]{:S(2)}, u32[]{:S(2)}) %collective-permute-start) | collective-permute-done | bytes 32800 | tf_op jit(solution)/shard_map/ppermute | solution.py:228
  100.6 4.1 %collective-permute-done.1 = f32[4,1024]{1,0:T(4,128)S(1)} collective-permute-done((f32[4,1024]{1,0:T(4,128)S(1)}, f32[4,1024]{1,0:T(4,128)S(1)}, u32[]{:S(2)}, u32[]{:S(2)}) %collective-permute-start.1) | collective-permute-done | bytes 16416 | tf_op jit(solution)/shard_map/ppermute | solution.py:228
  104.7 1.0 collective-permute-start.2
  105.8 1.8 collective-permute-done.2
  107.6 3.9 %collective-permute-start.3 = (f32[1,1024]{1,0:T(1,128)S(1)}, f32[1,1024]{1,0:T(1,128)S(1)}, u32[]{:S(2)}, u32[]{:S(2)}) collective-permute-start(f32[1,1024]{1,0:T(1,128)S(1)} %constant_dynamic-slice_fusion), channel_id=1, source_target_pairs={{0,16},{16,0},{32,48},{48,32},{64,80},{80,64},{96,112},{112,96},{1... | collective-permute-start | bytes 12296 | tf_op jit(solution)/shard_map/ppermute | solution.py:228
  111.5 2.2 select_convert_fusion
  113.7 1.9 copy-done.2
  115.6 1.0 copy-done.5
  116.7 1.0 copy-done.7
  117.7 10.5 %shard_map.114 = bf16[16,2,128,128]{3,2,1,0:T(8,128)(2,1)S(1)} custom-call(s32[1,2]{1,0:T(1,128)S(1)} %copy-done.9, bf16[16,6,128,128]{3,2,1,0:T(8,128)(2,1)S(1)} %copy-done.2, f32[4,128]{1,0:T(4,128)S(1)} %bitcast.22, bf16[2048,128]{1,0:T(8,128)(2,1)S(1)} %copy-done.7, bf16[2048,128]{1,0:T(8,128)(2,1)S(1)} %copy-done.5), custom_call_target="tpu_custom_call" | custom-call | flops 4294967296 | bytes 4194304 | tf_op jit(solution)/shard_map/pallas_call | solution.py:185
  129.2 35.8 %all-to-all-done.2.in_ref = bf16[16,6,128,128]{3,2,1,0:T(8,128)(2,1)S(1)} async-done(((bf16[16,6,128,128]{3,2,1,0:T(8,128)(2,1)}), bf16[16,6,128,128]{3,2,1,0:T(8,128)(2,1)S(1)}, u32[]{:S(2)}, u32[]{:S(2)}) %all-to-all-start.2) | async-done | bytes 3145760 | tf_op jit(solution)/shard_map/all_to_all | solution.py:200
  165.0 1.6 copy-done
  166.7 4.6 %all-to-all-start.1 = ((bf16[16,2,128,128]{3,2,1,0:T(8,128)(2,1)}), bf16[16,2,128,128]{3,2,1,0:T(8,128)(2,1)S(1)}, u32[]{:S(2)}, u32[]{:S(2)}) async-start(bf16[16,2,128,128]{3,2,1,0:T(8,128)(2,1)} %copy-done.3), calls=%async_computation.1 | async-start | bytes 2097152 | tf_op jit(solution)/shard_map/all_to_all | solution.py:200
  171.3 1.9 copy-done.1
  173.2 1.0 copy-done.6
  174.2 1.0 copy-done.8
  175.2 10.5 %shard_map.115 = bf16[16,2,128,128]{3,2,1,0:T(8,128)(2,1)S(1)} custom-call(s32[1,2]{1,0:T(1,128)S(1)} %copy-done.9, bf16[16,6,128,128]{3,2,1,0:T(8,128)(2,1)S(1)} %copy-done.1, f32[4,128]{1,0:T(4,128)S(1)} %bitcast.21, bf16[2048,128]{1,0:T(8,128)(2,1)S(1)} %copy-done.8, bf16[2048,128]{1,0:T(8,128)(2,1)S(1)} %copy-done.6), custom_call_target="tpu_custom_call" | custom-call | flops 4294967296 | bytes 4194304 | tf_op jit(solution)/shard_map/pallas_call | solution.py:185
  186.7 9.7 %all-to-all-done.1.refs_0_ = bf16[16,2,128,128]{3,2,1,0:T(8,128)(2,1)S(1)} async-done(((bf16[16,2,128,128]{3,2,1,0:T(8,128)(2,1)}), bf16[16,2,128,128]{3,2,1,0:T(8,128)(2,1)S(1)}, u32[]{:S(2)}, u32[]{:S(2)}) %all-to-all-start.1) | async-done | bytes 1048608 | tf_op jit(solution)/shard_map/all_to_all | solution.py:200
  196.4 33.5 %all_to_all.21.refs_1_ = bf16[16,2,128,128]{3,2,1,0:T(8,128)(2,1)S(1)} all-to-all(bf16[16,2,128,128]{3,2,1,0:T(8,128)(2,1)} %copy-done.4), channel_id=1, replica_groups=mesh['fsdp'=16,'seq'=16] {'seq'}, dimensions={0} | all-to-all | bytes 2097152 | tf_op jit(solution)/shard_map/all_to_all | solution.py:200
  229.9 2.0 shard_map.116
  (38 shorter events, 3.8 us)
Async XLA Ops:
  87.9 5.0 %copy-start.10 = (s32[16,2]{0,1:T(2,128)S(1)}, s32[16,2]{0,1:T(2,128)}, u32[]{:S(2)}) copy-start(s32[16,2]{0,1:T(2,128)} %param.18) | copy-start | bytes 388
  87.9 12.5 %copy-start.9 = (s32[1,2]{1,0:T(1,128)S(1)}, s32[1,2]{1,0:T(1,128)}, u32[]{:S(2)}) copy-start(s32[1,2]{1,0:T(1,128)} %len_ref.3) | copy-start | bytes 28
  87.9 77.1 %all-to-all-start.2 = ((bf16[16,6,128,128]{3,2,1,0:T(8,128)(2,1)}), bf16[16,6,128,128]{3,2,1,0:T(8,128)(2,1)S(1)}, u32[]{:S(2)}, u32[]{:S(2)}) async-start(bf16[16,6,128,128]{3,2,1,0:T(8,128)(2,1)} %get-tuple-element.5), calls=%async_computation.2 | async-start | bytes 6291456 | tf_op jit(solution)/shard_map/all_to_all | solution.py:200
  94.3 5.8 %collective-permute-start = (f32[8,1024]{1,0:T(8,128)S(1)}, f32[8,1024]{1,0:T(8,128)S(1)}, u32[]{:S(2)}, u32[]{:S(2)}) collective-permute-start(f32[8,1024]{1,0:T(8,128)S(1)} %dynamic-slice_bitcast_fusion), channel_id=1, source_target_pairs={{0,128},{16,144},{32,160},{48,176},{64,192},{80,208},{96,224},{112... | collective-permute-start | bytes 98312 | tf_op jit(solution)/shard_map/ppermute | solution.py:228
  100.2 4.5 %collective-permute-start.1 = (f32[4,1024]{1,0:T(4,128)S(1)}, f32[4,1024]{1,0:T(4,128)S(1)}, u32[]{:S(2)}, u32[]{:S(2)}) collective-permute-start(f32[4,1024]{1,0:T(4,128)S(1)} %dynamic-slice_bitcast_fusion.1), channel_id=1, source_target_pairs={{0,64},{16,80},{32,96},{48,112},{64,0},{80,16},{96,32},{112,48},{1... | collective-permute-start | bytes 49160 | tf_op jit(solution)/shard_map/ppermute | solution.py:228
  104.7 2.9 %collective-permute-start.2 = (f32[2,1024]{1,0:T(2,128)S(1)}, f32[2,1024]{1,0:T(2,128)S(1)}, u32[]{:S(2)}, u32[]{:S(2)}) collective-permute-start(f32[2,1024]{1,0:T(2,128)S(1)} %dynamic-slice_bitcast_fusion.2), channel_id=1, source_target_pairs={{0,32},{16,48},{32,0},{48,16},{64,96},{80,112},{96,64},{112,80},{1... | collective-permute-start | bytes 24584 | tf_op jit(solution)/shard_map/ppermute | solution.py:228
  107.6 6.1 %collective-permute-start.3 = (f32[1,1024]{1,0:T(1,128)S(1)}, f32[1,1024]{1,0:T(1,128)S(1)}, u32[]{:S(2)}, u32[]{:S(2)}) collective-permute-start(f32[1,1024]{1,0:T(1,128)S(1)} %constant_dynamic-slice_fusion), channel_id=1, source_target_pairs={{0,16},{16,0},{32,48},{48,32},{64,80},{80,64},{96,112},{112,96},{1... | collective-permute-start | bytes 12296 | tf_op jit(solution)/shard_map/ppermute | solution.py:228
  113.7 1.9 copy-start.2
  115.6 1.0 copy-start.5
  116.7 1.0 copy-start.7
  128.2 1.0 copy-start.3
  165.0 1.6 copy-start
  166.7 29.7 %all-to-all-start.1 = ((bf16[16,2,128,128]{3,2,1,0:T(8,128)(2,1)}), bf16[16,2,128,128]{3,2,1,0:T(8,128)(2,1)S(1)}, u32[]{:S(2)}, u32[]{:S(2)}) async-start(bf16[16,2,128,128]{3,2,1,0:T(8,128)(2,1)} %copy-done.3), calls=%async_computation.1 | async-start | bytes 2097152 | tf_op jit(solution)/shard_map/all_to_all | solution.py:200
  171.3 1.9 copy-start.1
  173.2 1.0 copy-start.6
  174.2 1.0 copy-start.8
  185.8 1.0 copy-start.4

commit v4 on v3

--- a/solution.py
+++ b/solution.py
@@ -17,32 +17,35 @@
 MIB = 1024 * 1024
 
 
-def pack_kernel(heads, *refs):
-    arrays, parts = refs[:-heads], refs[-heads:]
-    for place, ref in enumerate(arrays):
-        for group in range(GROUPS_A_STEP):
-            for head in range(heads):
-                column = (group * heads + head) * HDIM
-                parts[head][group, place] = ref[0, :, column : column + HDIM]
-
-
-def pack(arrays, heads):
+def pack_kernel(*refs):
+    part = refs[-1]
+    for index, ref in enumerate(refs[: ARRAYS * GROUPS_A_STEP]):
+        part[index % GROUPS_A_STEP, index // GROUPS_A_STEP] = ref[0]
+
+
+def pack_head(arrays, heads, head, *after):
     _, tokens, width = arrays[0].shape
     groups = width // (heads * HDIM)
     part = (ARRAYS, tokens, HDIM)
-    row_spec = pl.BlockSpec((1, tokens, GROUPS_A_STEP * heads * HDIM), lambda g: (0, 0, g))
-    part_spec = pl.BlockSpec((GROUPS_A_STEP,) + part, lambda g: (g, 0, 0, 0))
-    return pl.pallas_call(
-        functools.partial(pack_kernel, heads),
+
+    def column(turn):
+        def place(i):
+            return (0, 0, (i * GROUPS_A_STEP + turn) * heads + head)
+
+        return pl.BlockSpec((1, tokens, HDIM), place)
+
+    return pl.pallas_call(
+        pack_kernel,
         grid=(groups // GROUPS_A_STEP,),
-        in_specs=[row_spec] * ARRAYS,
-        out_specs=[part_spec] * heads,
-        out_shape=[jax.ShapeDtypeStruct((groups,) + part, jnp.bfloat16)] * heads,
-        compiler_params=pltpu.CompilerParams(vmem_limit_bytes=56 * MIB),
+        in_specs=[column(turn) for turn in range(GROUPS_A_STEP)] * ARRAYS
+        + [pl.BlockSpec(memory_space=pl.ANY)] * len(after),
+        out_specs=pl.BlockSpec((GROUPS_A_STEP,) + part, lambda i: (i, 0, 0, 0)),
+        out_shape=jax.ShapeDtypeStruct((groups,) + part, jnp.bfloat16),
+        compiler_params=pltpu.CompilerParams(vmem_limit_bytes=60 * MIB),
         cost_estimate=pl.CostEstimate(
-            flops=0, bytes_accessed=4 * ARRAYS * tokens * width, transcendentals=0
+            flops=0, bytes_accessed=4 * ARRAYS * groups * tokens * HDIM, transcendentals=0
         ),
-    )(*arrays)
+    )(*[array for array in arrays for _ in range(GROUPS_A_STEP)], *after)
 
 
 def unpack_kernel(*refs):
@@ -73,7 +76,7 @@
     )(*parts)
 
 
-def attention_kernel(len_ref, in_ref, gate_ref, query_side, key_side, out_ref):
+def attention_kernel(len_ref, in_ref, gate_ref, out_ref, query_side, key_side):
     groups, _, tokens, _ = in_ref.shape
     length = groups * tokens
     first_len = len_ref[0, 0]
@@ -83,6 +86,17 @@
     per = BLOCK // tokens
     blocks = length // BLOCK
     row = lax.broadcasted_iota(jnp.int32, (BLOCK, HDIM), 0)
+    lane = lax.broadcasted_iota(jnp.int32, (BLOCK, HDIM), 1)
+
+    def fill(block, carry):
+        start = pl.multiple_of(block * BLOCK, BLOCK)
+        own = jnp.where(start + row >= first_len, 1, 0)
+        rows = pl.ds(start, BLOCK)
+        query_side[rows, :] = jnp.where(lane == own, 1.0, 0.0).astype(jnp.bfloat16)
+        key_side[rows, :] = jnp.where(lane == 1 - own, MASKED, 0.0).astype(jnp.bfloat16)
+        return carry
+
+    lax.fori_loop(0, blocks, fill, 0)
 
     def rows_of(block, count, place):
         found = in_ref[pl.ds(block * per, count * per), place]
@@ -170,37 +184,30 @@
     lax.fori_loop(0, blocks, one_block, 0)
 
 
-def sides(first_len, length):
-    own = (jnp.arange(length, dtype=jnp.int32) >= first_len).astype(jnp.int32)[:, None]
-    lane = jnp.arange(HDIM, dtype=jnp.int32)[None, :]
-    query_side = jnp.where(lane == own, 1.0, 0.0).astype(jnp.bfloat16)
-    key_side = jnp.where(lane == 1 - own, MASKED, 0.0).astype(jnp.bfloat16)
-    return query_side, key_side
-
-
-def attend(lengths, received, gates, query_side, key_side):
+def attend(lengths, received, gates):
     groups, _, tokens, _ = received.shape
     length = groups * tokens
     in_vmem = pl.BlockSpec(memory_space=pltpu.VMEM)
     return pl.pallas_call(
         attention_kernel,
-        in_specs=[pl.BlockSpec(memory_space=pltpu.SMEM)] + [in_vmem] * 4,
+        in_specs=[pl.BlockSpec(memory_space=pltpu.SMEM)] + [in_vmem] * 2,
         out_specs=in_vmem,
         out_shape=jax.ShapeDtypeStruct((groups, 2, tokens, HDIM), jnp.bfloat16),
+        scratch_shapes=[pltpu.VMEM((length, HDIM), jnp.bfloat16)] * 2,
         compiler_params=pltpu.CompilerParams(vmem_limit_bytes=32 * MIB),
         cost_estimate=pl.CostEstimate(
             flops=8 * length * length * HDIM,
             bytes_accessed=16 * length * HDIM,
             transcendentals=length * length,
         ),
-    )(lengths, received, gates, query_side, key_side)
+    )(lengths, received, gates)
 
 
 def exchange(array):
     return lax.all_to_all(array, "seq", split_axis=0, concat_axis=0, tiled=True)
 
 
-def pick_gates(gate_table, rate_table, timesteps, groups):
+def pick_rows(gate_table, rate_table, timesteps, groups):
     steps_here, width = gate_table.shape
     here = width // groups
     column = lax.axis_index("seq") * here
@@ -211,24 +218,43 @@
         ],
         axis=1,
     )
-    me = lax.axis_index("fsdp")
-    wanted = timesteps.reshape(-1) - me * steps_here
+    wanted = timesteps.reshape(-1) - lax.axis_index("fsdp") * steps_here
     one_hot = (wanted[:, None] == jnp.arange(steps_here, dtype=jnp.int32)[None, :]).astype(
         jnp.float32
     )
     picks = jnp.dot(one_hot, tables, precision=lax.Precision.HIGHEST)
+    return picks.reshape(timesteps.shape[0], -1)
+
+
+def behind_kernel(array, after, out):
+    out[...] = array[...]
+
+
+def behind(array, after):
+    in_vmem = pl.BlockSpec(memory_space=pltpu.VMEM)
+    return pl.pallas_call(
+        behind_kernel,
+        in_specs=[in_vmem, pl.BlockSpec(memory_space=pl.ANY)],
+        out_specs=in_vmem,
+        out_shape=jax.ShapeDtypeStruct(array.shape, array.dtype),
+    )(array, after)
+
+
+def halve(picks, bit, members):
+    mine = (lax.axis_index("fsdp") // bit) % 2
+    split = picks.reshape(2, bit, -1)
+    kept = lax.dynamic_index_in_dim(split, mine, 0, keepdims=False)
+    sent = lax.dynamic_index_in_dim(split, 1 - mine, 0, keepdims=False)
+    return kept + lax.ppermute(sent, "fsdp", [(i, i ^ bit) for i in members])
+
+
+def sum_picks(picks, core):
     size = lax.axis_size("fsdp")
-    picks = picks.reshape(size, -1)
     bit = size // 2
-    while bit:
-        mine = (me // bit) % 2
-        halves = picks.reshape(2, bit, -1)
-        kept = lax.dynamic_index_in_dim(halves, mine, 0, keepdims=False)
-        sent = lax.dynamic_index_in_dim(halves, 1 - mine, 0, keepdims=False)
-        picks = kept + lax.ppermute(sent, "fsdp", [(i, i ^ bit) for i in range(size)])
+    while bit > 1:
+        picks = halve(picks, bit, range(core, size, 2))
         bit //= 2
-    mine = picks.reshape(2, 2, here // HDIM, HDIM)
-    return mine.transpose(2, 1, 0, 3).reshape(here // HDIM, 4, HDIM)
+    return picks
 
 
 def on_device(
@@ -246,13 +272,18 @@
     groups = lax.axis_size("seq")
     heads = queries.shape[2] // (groups * HDIM)
     arrays = (queries, key_states, value_states, query_tangent, key_tangent, value_tangent)
-    packed = pack(arrays, heads)
-    gates = pick_gates(gate_table, rate_table, timesteps, groups)
-    query_side, key_side = sides(lengths[0, 0], groups * queries.shape[1])
-    parts = []
-    for head in range(heads):
-        received = exchange(packed[head])
-        parts.append(attend(lengths, received, gates[head], query_side, key_side))
+    picks = pick_rows(gate_table, rate_table, timesteps, groups)
+    odd_sum = sum_picks(picks, 1)
+    packed = [pack_head(arrays, heads, 0, odd_sum)]
+    for head in range(1, heads):
+        packed.append(pack_head(arrays, heads, head, packed[-1]))
+    even_sum = sum_picks(behind(picks, packed[-1]), 0)
+    sums = jnp.where(lax.axis_index("fsdp") % 2 == 1, odd_sum, even_sum)
+    mine = halve(sums, 1, range(lax.axis_size("fsdp")))
+    mine = mine.reshape(2, 2, heads, HDIM)
+    gates = mine.transpose(2, 1, 0, 3).reshape(heads, 4, HDIM)
+    received = [exchange(part) for part in packed]
+    parts = [attend(lengths, array, gate) for array, gate in zip(received, gates)]
     return tuple(unpack([exchange(part) for part in parts]))
 
 

time: 234 us -> 220 us (0.940)
  blocking collectives: 115 us -> 96.3 us
  starting transfers between devices: 17.4 us -> 25.9 us
  local copies, waits for them, and re-layouts: 12.7 us -> 9.03 us
  waiting for transfers between devices: 54.5 us -> 51.1 us
  Pallas kernels: 29.2 us -> 31.6 us
    all_to_all x2, blocking collectives: 115 us -> 96.3 us  [exchange(): return lax.all_to_all(array, 'seq', split_axis=0, concat_axis=0, tiled=True)]
    unnamed x22 -> x12, local copies, waits for them, and re-layouts: 11.5 us -> 6.39 us
    all_to_all x2, starting transfers between devices: 9.54 us -> 14 us  [exchange(): return lax.all_to_all(array, 'seq', split_axis=0, concat_axis=0, tiled=True)]
    ppermute x4 -> x7, starting transfers between devices: 7.91 us -> 11.8 us  [halve(): return kept + lax.ppermute(sent, 'fsdp', [(i, i ^ bit) for i in members])]
    pallas_call x1 -> x3, Pallas kernels: 6.12 us -> 9.84 us  [the longest x2 8.37 us: pack_head(): pl.pallas_call(pack_kernel, grid=(groups // GROUPS_A_STEP,), in_specs=[co...]
    ppermute x4 -> x7, waiting for transfers between devices: 9 us -> 7.84 us  [halve(): return kept + lax.ppermute(sent, 'fsdp', [(i, i ^ bit) for i in members])]
  transfers between devices with their start and end apart: 6 -> 9, of which waited for: 5 -> 6; matrix products, arithmetic and copies ran while one was open for 2% -> 1% of each run, Pallas kernels for 9% -> 10%
where the time goes in v4:
time: 220 us; the launch traced here: 217 us
  blocking collectives  96.3 us (44%)
  waiting for transfers between devices  51.1 us (23%)
  Pallas kernels  31.6 us (14%)
  starting transfers between devices  25.9 us (12%)
  local copies, waits for them, and re-layouts  9.03 us (4%)
    all_to_all x2, blocking collectives, exchange(): return lax.all_to_all(array, 'seq', split_axis=0, concat_axis=0, tiled=True)  96.3 us
    all_to_all x2, waiting for transfers between devices, exchange(): return lax.all_to_all(array, 'seq', split_axis=0, concat_axis=0, tiled=True)  43.3 us
    pallas_call x2, Pallas kernels, attend(): pl.pallas_call(attention_kernel, in_specs=[pl.BlockSpec(memory_space=pltp...  19.7 us
    all_to_all x2, starting transfers between devices, exchange(): return lax.all_to_all(array, 'seq', split_axis=0, concat_axis=0, tiled=True)  14 us
    ppermute x7, starting transfers between devices, halve(): return kept + lax.ppermute(sent, 'fsdp', [(i, i ^ bit) for i in members])  11.8 us
    pallas_call x2, Pallas kernels, pack_head(): pl.pallas_call(pack_kernel, grid=(groups // GROUPS_A_STEP,), in_specs=[co...  8.37 us
    ppermute x7, waiting for transfers between devices, halve(): return kept + lax.ppermute(sent, 'fsdp', [(i, i ^ bit) for i in members])  7.84 us
    unnamed x12, local copies, waits for them, and re-layouts  6.39 us
  transfers between devices with their start and end apart: 9, of which 6 were waited for; matrix products, arithmetic and copies ran while one was open for 1% of the time, Pallas kernels for 10%

profile of v4, /device:TPU:5, one launch (start us, length us, event | category | flops | bytes accessed | tf_op | source)
XLA Modules:
  0.0 217.3 jit_solution(13506315042560352038)
XLA Ops:
  1.5 0.9 constant_dynamic-slice_fusion.1
  2.7 4.8 %collective-permute-start = (f32[8,1024]{1,0:T(8,128)S(1)}, f32[8,1024]{1,0:T(8,128)S(1)}, u32[]{:S(2)}, u32[]{:S(2)}) collective-permute-start(f32[8,1024]{1,0:T(8,128)S(1)} %dynamic-slice_bitcast_fusion.1), channel_id=1, source_target_pairs={{16,144},{48,176},{80,208},{112,240},{144,16},{176,48},{208,80},{2... | collective-permute-start | bytes 98312 | tf_op jit(solution)/shard_map/ppermute | solution.py:248
  7.6 1.3 collective-permute-done
  8.9 2.1 collective-permute-start.1
  11.0 3.8 %collective-permute-done.1 = f32[4,1024]{1,0:T(4,128)S(1)} collective-permute-done((f32[4,1024]{1,0:T(4,128)S(1)}, f32[4,1024]{1,0:T(4,128)S(1)}, u32[]{:S(2)}, u32[]{:S(2)}) %collective-permute-start.1) | collective-permute-done | bytes 16416 | tf_op jit(solution)/shard_map/ppermute | solution.py:248
  14.9 2.8 %collective-permute-start.2 = (f32[2,1024]{1,0:T(2,128)S(1)}, f32[2,1024]{1,0:T(2,128)S(1)}, u32[]{:S(2)}, u32[]{:S(2)}) collective-permute-start(f32[2,1024]{1,0:T(2,128)S(1)} %dynamic-slice_bitcast_fusion.5), channel_id=1, source_target_pairs={{16,48},{48,16},{80,112},{112,80},{144,176},{176,144},{208,240},{2... | collective-permute-start | bytes 24584 | tf_op jit(solution)/shard_map/ppermute | solution.py:248
  17.8 1.6 collective-permute-done.2
  19.9 4.1 %shard_map.113.refs_24_ = bf16[16,6,128,128]{3,2,1,0:T(8,128)(2,1)} custom-call(bf16[1,128,4096]{2,1,0:T(8,128)(2,1)} %refs_3_.3, bf16[1,128,4096]{2,1,0:T(8,128)(2,1)} %refs_3_.3, bf16[1,128,4096]{2,1,0:T(8,128)(2,1)} %refs_3_.3, bf16[1,128,4096]{2,1,0:T(8,128)(2,1)} %refs_3_.3, bf16[1,128,4096]{2,1,0:T(8,128)(2,1)} %refs_7_.3, ...), custom_call_target="tpu_custom_call" | custom-call | bytes 6291456 | tf_op jit(solution)/shard_map/pallas_call | solution.py:37
  24.1 4.2 %shard_map.114.after = bf16[16,6,128,128]{3,2,1,0:T(8,128)(2,1)} custom-call(bf16[1,128,4096]{2,1,0:T(8,128)(2,1)} %refs_3_.3, bf16[1,128,4096]{2,1,0:T(8,128)(2,1)} %refs_3_.3, bf16[1,128,4096]{2,1,0:T(8,128)(2,1)} %refs_3_.3, bf16[1,128,4096]{2,1,0:T(8,128)(2,1)} %refs_3_.3, bf16[1,128,4096]{2,1,0:T(8,128)(2,1)} %refs_7_.3, bf16[1,128,4096]{2,1,0:T(8,128)(2,1)} %refs_7_.3, ...), custom_call_target="tpu_custom_call" | custom-call | bytes 6291456 | tf_op jit(solution)/shard_map/pallas_call | solution.py:37
  28.3 70.2 %all_to_all.20.in_ref = bf16[16,6,128,128]{3,2,1,0:T(8,128)(2,1)} all-to-all(bf16[16,6,128,128]{3,2,1,0:T(8,128)(2,1)} %shard_map.114.after), channel_id=1, replica_groups=mesh['fsdp'=16,'seq'=16] {'seq'}, dimensions={0} | all-to-all | bytes 6291456 | tf_op jit(solution)/shard_map/all_to_all | solution.py:207
  98.5 10.2 %all-to-all-start = ((bf16[16,6,128,128]{3,2,1,0:T(8,128)(2,1)}), bf16[16,6,128,128]{3,2,1,0:T(8,128)(2,1)S(1)}, u32[]{:S(2)}, u32[]{:S(2)}) async-start(bf16[16,6,128,128]{3,2,1,0:T(8,128)(2,1)} %shard_map.113.refs_24_), calls=%async_computation | async-start | bytes 6291456 | tf_op jit(solution)/shard_map/all_to_all | solution.py:207
  109.4 1.5 shard_map.115
  114.7 1.1 collective-permute-done.6
  115.9 1.9 copy-done.2
  117.8 10.0 %shard_map.117 = bf16[16,2,128,128]{3,2,1,0:T(8,128)(2,1)S(1)} custom-call(s32[1,2]{1,0:T(1,128)S(1)} %copy-done.4, bf16[16,6,128,128]{3,2,1,0:T(8,128)(2,1)S(1)} %copy-done.2, f32[4,128]{1,0:T(4,128)S(1)} %bitcast.34), custom_call_target="tpu_custom_call" | custom-call | flops 4294967296 | bytes 4194304 | tf_op jit(solution)/shard_map/pallas_call | solution.py:191
  127.8 1.0 copy-done.3
  128.8 36.8 %all-to-all-done.in_ref = bf16[16,6,128,128]{3,2,1,0:T(8,128)(2,1)S(1)} async-done(((bf16[16,6,128,128]{3,2,1,0:T(8,128)(2,1)}), bf16[16,6,128,128]{3,2,1,0:T(8,128)(2,1)S(1)}, u32[]{:S(2)}, u32[]{:S(2)}) %all-to-all-start) | async-done | bytes 3145760 | tf_op jit(solution)/shard_map/all_to_all | solution.py:207
  165.5 1.6 copy-done
  167.2 3.8 %all-to-all-start.3 = ((bf16[16,2,128,128]{3,2,1,0:T(8,128)(2,1)}), bf16[16,2,128,128]{3,2,1,0:T(8,128)(2,1)S(1)}, u32[]{:S(2)}, u32[]{:S(2)}) async-start(bf16[16,2,128,128]{3,2,1,0:T(8,128)(2,1)} %copy-done.3), calls=%async_computation.3 | async-start | bytes 2097152 | tf_op jit(solution)/shard_map/all_to_all | solution.py:207
  171.0 1.9 copy-done.1
  172.9 9.7 %shard_map.116 = bf16[16,2,128,128]{3,2,1,0:T(8,128)(2,1)S(1)} custom-call(s32[1,2]{1,0:T(1,128)S(1)} %copy-done.4, bf16[16,6,128,128]{3,2,1,0:T(8,128)(2,1)S(1)} %copy-done.1, f32[4,128]{1,0:T(4,128)S(1)} %bitcast.33), custom_call_target="tpu_custom_call" | custom-call | flops 4294967296 | bytes 4194304 | tf_op jit(solution)/shard_map/pallas_call | solution.py:191
  182.6 6.5 %all-to-all-done.3.refs_1_ = bf16[16,2,128,128]{3,2,1,0:T(8,128)(2,1)S(1)} async-done(((bf16[16,2,128,128]{3,2,1,0:T(8,128)(2,1)}), bf16[16,2,128,128]{3,2,1,0:T(8,128)(2,1)S(1)}, u32[]{:S(2)}, u32[]{:S(2)}) %all-to-all-start.3) | async-done | bytes 1048608 | tf_op jit(solution)/shard_map/all_to_all | solution.py:207
  189.2 26.1 %all_to_all.21.refs_0_ = bf16[16,2,128,128]{3,2,1,0:T(8,128)(2,1)S(1)} all-to-all(bf16[16,2,128,128]{3,2,1,0:T(8,128)(2,1)S(1)} %shard_map.116), channel_id=1, replica_groups=mesh['fsdp'=16,'seq'=16] {'seq'}, dimensions={0} | all-to-all | bytes 2097152 | tf_op jit(solution)/shard_map/all_to_all | solution.py:207
  215.3 2.0 shard_map.118
  (41 shorter events, 6.2 us)
Async XLA Ops:
  2.7 6.2 %collective-permute-start = (f32[8,1024]{1,0:T(8,128)S(1)}, f32[8,1024]{1,0:T(8,128)S(1)}, u32[]{:S(2)}, u32[]{:S(2)}) collective-permute-start(f32[8,1024]{1,0:T(8,128)S(1)} %dynamic-slice_bitcast_fusion.1), channel_id=1, source_target_pairs={{16,144},{48,176},{80,208},{112,240},{144,16},{176,48},{208,80},{2... | collective-permute-start | bytes 98312 | tf_op jit(solution)/shard_map/ppermute | solution.py:248
  8.9 6.0 %collective-permute-start.1 = (f32[4,1024]{1,0:T(4,128)S(1)}, f32[4,1024]{1,0:T(4,128)S(1)}, u32[]{:S(2)}, u32[]{:S(2)}) collective-permute-start(f32[4,1024]{1,0:T(4,128)S(1)} %dynamic-slice_bitcast_fusion.3), channel_id=1, source_target_pairs={{16,80},{48,112},{80,16},{112,48},{144,208},{176,240},{208,144},{2... | collective-permute-start | bytes 49160 | tf_op jit(solution)/shard_map/ppermute | solution.py:248
  14.9 4.4 %collective-permute-start.2 = (f32[2,1024]{1,0:T(2,128)S(1)}, f32[2,1024]{1,0:T(2,128)S(1)}, u32[]{:S(2)}, u32[]{:S(2)}) collective-permute-start(f32[2,1024]{1,0:T(2,128)S(1)} %dynamic-slice_bitcast_fusion.5), channel_id=1, source_target_pairs={{16,48},{48,16},{80,112},{112,80},{144,176},{176,144},{208,240},{2... | collective-permute-start | bytes 24584 | tf_op jit(solution)/shard_map/ppermute | solution.py:248
  98.5 67.0 %all-to-all-start = ((bf16[16,6,128,128]{3,2,1,0:T(8,128)(2,1)}), bf16[16,6,128,128]{3,2,1,0:T(8,128)(2,1)S(1)}, u32[]{:S(2)}, u32[]{:S(2)}) async-start(bf16[16,6,128,128]{3,2,1,0:T(8,128)(2,1)} %shard_map.113.refs_24_), calls=%async_computation | async-start | bytes 6291456 | tf_op jit(solution)/shard_map/all_to_all | solution.py:207
  108.7 5.8 %copy-start.5 = (f32[2,1024]{1,0:T(2,128)S(1)}, f32[2,1024]{1,0:T(2,128)}, u32[]{:S(2)}) copy-start(f32[2,1024]{1,0:T(2,128)} %bitcast_add_fusion.5.refs_24_) | copy-start | bytes 24580
  108.7 7.2 %copy-start.4 = (s32[1,2]{1,0:T(1,128)S(1)}, s32[1,2]{1,0:T(1,128)}, u32[]{:S(2)}) copy-start(s32[1,2]{1,0:T(1,128)} %len_ref.3) | copy-start | bytes 28
  111.6 0.7 collective-permute-start.3
  113.1 0.7 collective-permute-start.4
  113.9 0.7 collective-permute-start.5
  114.6 1.3 collective-permute-start.6
  115.9 1.9 copy-start.2
  127.8 1.0 copy-start.3
  165.5 1.6 copy-start
  167.2 22.0 %all-to-all-start.3 = ((bf16[16,2,128,128]{3,2,1,0:T(8,128)(2,1)}), bf16[16,2,128,128]{3,2,1,0:T(8,128)(2,1)S(1)}, u32[]{:S(2)}, u32[]{:S(2)}) async-start(bf16[16,2,128,128]{3,2,1,0:T(8,128)(2,1)} %copy-done.3), calls=%async_computation.3 | async-start | bytes 2097152 | tf_op jit(solution)/shard_map/all_to_all | solution.py:207
  171.0 1.9 copy-start.1

commit v5 on v4

--- a/solution.py
+++ b/solution.py
@@ -17,35 +17,32 @@
 MIB = 1024 * 1024
 
 
-def pack_kernel(*refs):
-    part = refs[-1]
-    for index, ref in enumerate(refs[: ARRAYS * GROUPS_A_STEP]):
-        part[index % GROUPS_A_STEP, index // GROUPS_A_STEP] = ref[0]
-
-
-def pack_head(arrays, heads, head, *after):
+def pack_kernel(heads, *refs):
+    parts = refs[-heads:]
+    for place, ref in enumerate(refs[:ARRAYS]):
+        for group in range(GROUPS_A_STEP):
+            for head in range(heads):
+                column = (group * heads + head) * HDIM
+                parts[head][group, place] = ref[0, :, column : column + HDIM]
+
+
+def pack(arrays, heads, *after):
     _, tokens, width = arrays[0].shape
     groups = width // (heads * HDIM)
     part = (ARRAYS, tokens, HDIM)
-
-    def column(turn):
-        def place(i):
-            return (0, 0, (i * GROUPS_A_STEP + turn) * heads + head)
-
-        return pl.BlockSpec((1, tokens, HDIM), place)
-
-    return pl.pallas_call(
-        pack_kernel,
+    row_spec = pl.BlockSpec((1, tokens, GROUPS_A_STEP * heads * HDIM), lambda g: (0, 0, g))
+    part_spec = pl.BlockSpec((GROUPS_A_STEP,) + part, lambda g: (g, 0, 0, 0))
+    return pl.pallas_call(
+        functools.partial(pack_kernel, heads),
         grid=(groups // GROUPS_A_STEP,),
-        in_specs=[column(turn) for turn in range(GROUPS_A_STEP)] * ARRAYS
-        + [pl.BlockSpec(memory_space=pl.ANY)] * len(after),
-        out_specs=pl.BlockSpec((GROUPS_A_STEP,) + part, lambda i: (i, 0, 0, 0)),
-        out_shape=jax.ShapeDtypeStruct((groups,) + part, jnp.bfloat16),
-        compiler_params=pltpu.CompilerParams(vmem_limit_bytes=60 * MIB),
+        in_specs=[row_spec] * ARRAYS + [pl.BlockSpec(memory_space=pl.ANY)] * len(after),
+        out_specs=[part_spec] * heads,
+        out_shape=[jax.ShapeDtypeStruct((groups,) + part, jnp.bfloat16)] * heads,
+        compiler_params=pltpu.CompilerParams(vmem_limit_bytes=56 * MIB),
         cost_estimate=pl.CostEstimate(
-            flops=0, bytes_accessed=4 * ARRAYS * groups * tokens * HDIM, transcendentals=0
+            flops=0, bytes_accessed=4 * ARRAYS * tokens * width, transcendentals=0
         ),
-    )(*[array for array in arrays for _ in range(GROUPS_A_STEP)], *after)
+    )(*arrays, *after)
 
 
 def unpack_kernel(*refs):
@@ -274,9 +271,7 @@
     arrays = (queries, key_states, value_states, query_tangent, key_tangent, value_tangent)
     picks = pick_rows(gate_table, rate_table, timesteps, groups)
     odd_sum = sum_picks(picks, 1)
-    packed = [pack_head(arrays, heads, 0, odd_sum)]
-    for head in range(1, heads):
-        packed.append(pack_head(arrays, heads, head, packed[-1]))
+    packed = pack(arrays, heads, odd_sum)
     even_sum = sum_picks(behind(picks, packed[-1]), 0)
     sums = jnp.where(lax.axis_index("fsdp") % 2 == 1, odd_sum, even_sum)
     mine = halve(sums, 1, range(lax.axis_size("fsdp")))

time: 220 us -> 217 us (0.986)
    pallas_call x2 -> x1, Pallas kernels: 8.37 us -> 6.16 us  [pack(): pl.pallas_call(functools.partial(pack_kernel, heads), grid=(groups // GRO...]
  transfers between devices with their start and end apart: 9 -> 9, of which waited for: 6 -> 6; matrix products, arithmetic and copies ran while one was open for 1% -> 1% of each run, Pallas kernels for 10% -> 11%
where the time goes in v5:
time: 217 us; the launch traced here: 215 us
  blocking collectives  96.3 us (44%)
  waiting for transfers between devices  49.3 us (23%)
  Pallas kernels  31.2 us (14%)
  starting transfers between devices  25.9 us (12%)
  local copies, waits for them, and re-layouts  9.03 us (4%)
    all_to_all x2, blocking collectives, exchange(): return lax.all_to_all(array, 'seq', split_axis=0, concat_axis=0, tiled=True)  96.3 us
    all_to_all x2, waiting for transfers between devices, exchange(): return lax.all_to_all(array, 'seq', split_axis=0, concat_axis=0, tiled=True)  41.5 us
    pallas_call x2, Pallas kernels, attend(): pl.pallas_call(attention_kernel, in_specs=[pl.BlockSpec(memory_space=pltp...  21.5 us
    all_to_all x2, starting transfers between devices, exchange(): return lax.all_to_all(array, 'seq', split_axis=0, concat_axis=0, tiled=True)  14 us
    ppermute x7, starting transfers between devices, halve(): return kept + lax.ppermute(sent, 'fsdp', [(i, i ^ bit) for i in members])  11.8 us
    ppermute x7, waiting for transfers between devices, halve(): return kept + lax.ppermute(sent, 'fsdp', [(i, i ^ bit) for i in members])  7.84 us
    unnamed x12, local copies, waits for them, and re-layouts  6.38 us
    pallas_call x1, Pallas kernels, pack(): pl.pallas_call(functools.partial(pack_kernel, heads), grid=(groups // GRO...  6.16 us
  transfers between devices with their start and end apart: 9, of which 6 were waited for; matrix products, arithmetic and copies ran while one was open for 1% of the time, Pallas kernels for 11%

profile of v5, /device:TPU:5, one launch (start us, length us, event | category | flops | bytes accessed | tf_op | source)
XLA Modules:
  0.0 215.1 jit_solution(1202547165055031101)
XLA Ops:
  1.5 0.9 constant_dynamic-slice_fusion.1
  2.7 4.8 %collective-permute-start = (f32[8,1024]{1,0:T(8,128)S(1)}, f32[8,1024]{1,0:T(8,128)S(1)}, u32[]{:S(2)}, u32[]{:S(2)}) collective-permute-start(f32[8,1024]{1,0:T(8,128)S(1)} %dynamic-slice_bitcast_fusion.1), channel_id=1, source_target_pairs={{16,144},{48,176},{80,208},{112,240},{144,16},{176,48},{208,80},{2... | collective-permute-start | bytes 98312 | tf_op jit(solution)/shard_map/ppermute | solution.py:245
  7.6 1.3 collective-permute-done
  8.9 2.1 collective-permute-start.1
  11.0 3.8 %collective-permute-done.1 = f32[4,1024]{1,0:T(4,128)S(1)} collective-permute-done((f32[4,1024]{1,0:T(4,128)S(1)}, f32[4,1024]{1,0:T(4,128)S(1)}, u32[]{:S(2)}, u32[]{:S(2)}) %collective-permute-start.1) | collective-permute-done | bytes 16416 | tf_op jit(solution)/shard_map/ppermute | solution.py:245
  14.9 2.8 %collective-permute-start.2 = (f32[2,1024]{1,0:T(2,128)S(1)}, f32[2,1024]{1,0:T(2,128)S(1)}, u32[]{:S(2)}, u32[]{:S(2)}) collective-permute-start(f32[2,1024]{1,0:T(2,128)S(1)} %dynamic-slice_bitcast_fusion.5), channel_id=1, source_target_pairs={{16,48},{48,16},{80,112},{112,80},{144,176},{176,144},{208,240},{2... | collective-permute-start | bytes 24584 | tf_op jit(solution)/shard_map/ppermute | solution.py:245
  17.8 1.6 collective-permute-done.2
  19.9 6.2 %shard_map.113 = (bf16[16,6,128,128]{3,2,1,0:T(8,128)(2,1)}, bf16[16,6,128,128]{3,2,1,0:T(8,128)(2,1)}) custom-call(bf16[1,128,4096]{2,1,0:T(8,128)(2,1)} %refs_0_.1, bf16[1,128,4096]{2,1,0:T(8,128)(2,1)} %refs_1_.1, bf16[1,128,4096]{2,1,0:T(8,128)(2,1)} %refs_2_.1, bf16[1,128,4096]{2,1,0:T(8,128)(2,1)} %refs_3_.1, bf16[1,128,4096]{2,1,0:T(8,128)(2,1)} %refs_4_.1, ...), custom_call_target="tpu_custom_call" | custom-call | bytes 12582912 | tf_op jit(solution)/shard_map/pallas_call | solution.py:35
  26.1 70.2 %all_to_all.20.in_ref = bf16[16,6,128,128]{3,2,1,0:T(8,128)(2,1)} all-to-all(bf16[16,6,128,128]{3,2,1,0:T(8,128)(2,1)} %get-tuple-element.5.after), channel_id=1, replica_groups=mesh['fsdp'=16,'seq'=16] {'seq'}, dimensions={0} | all-to-all | bytes 6291456 | tf_op jit(solution)/shard_map/all_to_all | solution.py:204
  96.3 10.2 %all-to-all-start = ((bf16[16,6,128,128]{3,2,1,0:T(8,128)(2,1)}), bf16[16,6,128,128]{3,2,1,0:T(8,128)(2,1)S(1)}, u32[]{:S(2)}, u32[]{:S(2)}) async-start(bf16[16,6,128,128]{3,2,1,0:T(8,128)(2,1)} %get-tuple-element.4), calls=%async_computation | async-start | bytes 6291456 | tf_op jit(solution)/shard_map/all_to_all | solution.py:204
  107.2 1.5 shard_map.114
  110.1 0.8 bitcast_add_fusion
  112.5 1.1 collective-permute-done.6
  113.7 1.9 copy-done.2
  115.6 10.9 %shard_map.116 = bf16[16,2,128,128]{3,2,1,0:T(8,128)(2,1)S(1)} custom-call(s32[1,2]{1,0:T(1,128)S(1)} %copy-done.4, bf16[16,6,128,128]{3,2,1,0:T(8,128)(2,1)S(1)} %copy-done.2, f32[4,128]{1,0:T(4,128)S(1)} %bitcast.34), custom_call_target="tpu_custom_call" | custom-call | flops 4294967296 | bytes 4194304 | tf_op jit(solution)/shard_map/pallas_call | solution.py:188
  126.5 1.0 copy-done.3
  127.5 35.9 %all-to-all-done.in_ref = bf16[16,6,128,128]{3,2,1,0:T(8,128)(2,1)S(1)} async-done(((bf16[16,6,128,128]{3,2,1,0:T(8,128)(2,1)}), bf16[16,6,128,128]{3,2,1,0:T(8,128)(2,1)S(1)}, u32[]{:S(2)}, u32[]{:S(2)}) %all-to-all-start) | async-done | bytes 3145760 | tf_op jit(solution)/shard_map/all_to_all | solution.py:204
  163.3 1.6 copy-done
  165.0 3.8 %all-to-all-start.3 = ((bf16[16,2,128,128]{3,2,1,0:T(8,128)(2,1)}), bf16[16,2,128,128]{3,2,1,0:T(8,128)(2,1)S(1)}, u32[]{:S(2)}, u32[]{:S(2)}) async-start(bf16[16,2,128,128]{3,2,1,0:T(8,128)(2,1)} %copy-done.3), calls=%async_computation.3 | async-start | bytes 2097152 | tf_op jit(solution)/shard_map/all_to_all | solution.py:204
  168.8 1.9 copy-done.1
  170.7 10.6 %shard_map.115 = bf16[16,2,128,128]{3,2,1,0:T(8,128)(2,1)S(1)} custom-call(s32[1,2]{1,0:T(1,128)S(1)} %copy-done.4, bf16[16,6,128,128]{3,2,1,0:T(8,128)(2,1)S(1)} %copy-done.1, f32[4,128]{1,0:T(4,128)S(1)} %bitcast.33), custom_call_target="tpu_custom_call" | custom-call | flops 4294967296 | bytes 4194304 | tf_op jit(solution)/shard_map/pallas_call | solution.py:188
  181.3 5.6 %all-to-all-done.3.refs_1_ = bf16[16,2,128,128]{3,2,1,0:T(8,128)(2,1)S(1)} async-done(((bf16[16,2,128,128]{3,2,1,0:T(8,128)(2,1)}), bf16[16,2,128,128]{3,2,1,0:T(8,128)(2,1)S(1)}, u32[]{:S(2)}, u32[]{:S(2)}) %all-to-all-start.3) | async-done | bytes 1048608 | tf_op jit(solution)/shard_map/all_to_all | solution.py:204
  186.9 26.1 %all_to_all.21.refs_0_ = bf16[16,2,128,128]{3,2,1,0:T(8,128)(2,1)S(1)} all-to-all(bf16[16,2,128,128]{3,2,1,0:T(8,128)(2,1)S(1)} %shard_map.115), channel_id=1, replica_groups=mesh['fsdp'=16,'seq'=16] {'seq'}, dimensions={0} | all-to-all | bytes 2097152 | tf_op jit(solution)/shard_map/all_to_all | solution.py:204
  213.0 2.0 shard_map.117
  (40 shorter events, 5.4 us)
Async XLA Ops:
  2.7 6.2 %collective-permute-start = (f32[8,1024]{1,0:T(8,128)S(1)}, f32[8,1024]{1,0:T(8,128)S(1)}, u32[]{:S(2)}, u32[]{:S(2)}) collective-permute-start(f32[8,1024]{1,0:T(8,128)S(1)} %dynamic-slice_bitcast_fusion.1), channel_id=1, source_target_pairs={{16,144},{48,176},{80,208},{112,240},{144,16},{176,48},{208,80},{2... | collective-permute-start | bytes 98312 | tf_op jit(solution)/shard_map/ppermute | solution.py:245
  8.9 6.0 %collective-permute-start.1 = (f32[4,1024]{1,0:T(4,128)S(1)}, f32[4,1024]{1,0:T(4,128)S(1)}, u32[]{:S(2)}, u32[]{:S(2)}) collective-permute-start(f32[4,1024]{1,0:T(4,128)S(1)} %dynamic-slice_bitcast_fusion.3), channel_id=1, source_target_pairs={{16,80},{48,112},{80,16},{112,48},{144,208},{176,240},{208,144},{2... | collective-permute-start | bytes 49160 | tf_op jit(solution)/shard_map/ppermute | solution.py:245
  14.9 4.4 %collective-permute-start.2 = (f32[2,1024]{1,0:T(2,128)S(1)}, f32[2,1024]{1,0:T(2,128)S(1)}, u32[]{:S(2)}, u32[]{:S(2)}) collective-permute-start(f32[2,1024]{1,0:T(2,128)S(1)} %dynamic-slice_bitcast_fusion.5), channel_id=1, source_target_pairs={{16,48},{48,16},{80,112},{112,80},{144,176},{176,144},{208,240},{2... | collective-permute-start | bytes 24584 | tf_op jit(solution)/shard_map/ppermute | solution.py:245
  96.3 67.0 %all-to-all-start = ((bf16[16,6,128,128]{3,2,1,0:T(8,128)(2,1)}), bf16[16,6,128,128]{3,2,1,0:T(8,128)(2,1)S(1)}, u32[]{:S(2)}, u32[]{:S(2)}) async-start(bf16[16,6,128,128]{3,2,1,0:T(8,128)(2,1)} %get-tuple-element.4), calls=%async_computation | async-start | bytes 6291456 | tf_op jit(solution)/shard_map/all_to_all | solution.py:204
  106.5 5.8 %copy-start.5 = (f32[2,1024]{1,0:T(2,128)S(1)}, f32[2,1024]{1,0:T(2,128)}, u32[]{:S(2)}) copy-start(f32[2,1024]{1,0:T(2,128)} %bitcast_add_fusion.5.refs_6_) | copy-start | bytes 24580
  106.5 7.2 %copy-start.4 = (s32[1,2]{1,0:T(1,128)S(1)}, s32[1,2]{1,0:T(1,128)}, u32[]{:S(2)}) copy-start(s32[1,2]{1,0:T(1,128)} %len_ref.3) | copy-start | bytes 28
  109.4 0.7 collective-permute-start.3
  110.9 0.7 collective-permute-start.4
  111.6 0.7 collective-permute-start.5
  112.4 1.3 collective-permute-start.6
  113.7 1.9 copy-start.2
  126.5 1.0 copy-start.3
  163.3 1.6 copy-start
  165.0 22.0 %all-to-all-start.3 = ((bf16[16,2,128,128]{3,2,1,0:T(8,128)(2,1)}), bf16[16,2,128,128]{3,2,1,0:T(8,128)(2,1)S(1)}, u32[]{:S(2)}, u32[]{:S(2)}) async-start(bf16[16,2,128,128]{3,2,1,0:T(8,128)(2,1)} %copy-done.3), calls=%async_computation.3 | async-start | bytes 2097152 | tf_op jit(solution)/shard_map/all_to_all | solution.py:204
  168.8 1.9 copy-start.1

commit v6 on v5

--- a/solution.py
+++ b/solution.py
@@ -10,7 +10,7 @@
 
 HDIM = 128
 BLOCK = 256
-GROUPS_A_STEP = 4
+GROUPS_A_STEP = 8
 ARRAYS = 6
 MASKED = -1e30
 WIDTHS = (2, 3, 4, 5, 6)

time: 217 us -> 215 us (level)
  Pallas kernels: 31.2 us -> 27.8 us
  transfers between devices with their start and end apart: 9 -> 9, of which waited for: 6 -> 6; matrix products, arithmetic and copies ran while one was open for 1% -> 1% of each run, Pallas kernels for 11% -> 10%
where the time goes in v6:
time: 215 us; the launch traced here: 214 us
  blocking collectives  96.3 us (45%)
  waiting for transfers between devices  51.2 us (24%)
  Pallas kernels  27.8 us (13%)
  starting transfers between devices  25.9 us (12%)
  local copies, waits for them, and re-layouts  9.03 us (4%)
    all_to_all x2, blocking collectives, exchange(): return lax.all_to_all(array, 'seq', split_axis=0, concat_axis=0, tiled=True)  96.3 us
    all_to_all x2, waiting for transfers between devices, exchange(): return lax.all_to_all(array, 'seq', split_axis=0, concat_axis=0, tiled=True)  43.3 us
    pallas_call x2, Pallas kernels, attend(): pl.pallas_call(attention_kernel, in_specs=[pl.BlockSpec(memory_space=pltp...  19.7 us
    all_to_all x2, starting transfers between devices, exchange(): return lax.all_to_all(array, 'seq', split_axis=0, concat_axis=0, tiled=True)  14 us
    ppermute x7, starting transfers between devices, halve(): return kept + lax.ppermute(sent, 'fsdp', [(i, i ^ bit) for i in members])  11.8 us
    ppermute x7, waiting for transfers between devices, halve(): return kept + lax.ppermute(sent, 'fsdp', [(i, i ^ bit) for i in members])  7.84 us
    unnamed x12, local copies, waits for them, and re-layouts  6.38 us
    pallas_call x1, Pallas kernels, pack(): pl.pallas_call(functools.partial(pack_kernel, heads), grid=(groups // GRO...  5.08 us
  transfers between devices with their start and end apart: 9, of which 6 were waited for; matrix products, arithmetic and copies ran while one was open for 1% of the time, Pallas kernels for 10%

profile of v6, /device:TPU:5, one launch (start us, length us, event | category | flops | bytes accessed | tf_op | source)
XLA Modules:
  0.0 213.6 jit_solution(18061377860277254272)
XLA Ops:
  1.5 0.9 constant_dynamic-slice_fusion.1
  2.7 4.8 %collective-permute-start = (f32[8,1024]{1,0:T(8,128)S(1)}, f32[8,1024]{1,0:T(8,128)S(1)}, u32[]{:S(2)}, u32[]{:S(2)}) collective-permute-start(f32[8,1024]{1,0:T(8,128)S(1)} %dynamic-slice_bitcast_fusion.1), channel_id=1, source_target_pairs={{16,144},{48,176},{80,208},{112,240},{144,16},{176,48},{208,80},{2... | collective-permute-start | bytes 98312 | tf_op jit(solution)/shard_map/ppermute | solution.py:245
  7.6 1.3 collective-permute-done
  8.9 2.1 collective-permute-start.1
  11.0 3.8 %collective-permute-done.1 = f32[4,1024]{1,0:T(4,128)S(1)} collective-permute-done((f32[4,1024]{1,0:T(4,128)S(1)}, f32[4,1024]{1,0:T(4,128)S(1)}, u32[]{:S(2)}, u32[]{:S(2)}) %collective-permute-start.1) | collective-permute-done | bytes 16416 | tf_op jit(solution)/shard_map/ppermute | solution.py:245
  14.9 2.8 %collective-permute-start.2 = (f32[2,1024]{1,0:T(2,128)S(1)}, f32[2,1024]{1,0:T(2,128)S(1)}, u32[]{:S(2)}, u32[]{:S(2)}) collective-permute-start(f32[2,1024]{1,0:T(2,128)S(1)} %dynamic-slice_bitcast_fusion.5), channel_id=1, source_target_pairs={{16,48},{48,16},{80,112},{112,80},{144,176},{176,144},{208,240},{2... | collective-permute-start | bytes 24584 | tf_op jit(solution)/shard_map/ppermute | solution.py:245
  17.8 1.6 collective-permute-done.2
  19.9 5.1 %shard_map.113 = (bf16[16,6,128,128]{3,2,1,0:T(8,128)(2,1)}, bf16[16,6,128,128]{3,2,1,0:T(8,128)(2,1)}) custom-call(bf16[1,128,4096]{2,1,0:T(8,128)(2,1)} %refs_0_.1, bf16[1,128,4096]{2,1,0:T(8,128)(2,1)} %refs_1_.1, bf16[1,128,4096]{2,1,0:T(8,128)(2,1)} %refs_2_.1, bf16[1,128,4096]{2,1,0:T(8,128)(2,1)} %refs_3_.1, bf16[1,128,4096]{2,1,0:T(8,128)(2,1)} %refs_4_.1, ...), custom_call_target="tpu_custom_call" | custom-call | bytes 12582912 | tf_op jit(solution)/shard_map/pallas_call | solution.py:35
  25.0 70.2 %all_to_all.20.in_ref = bf16[16,6,128,128]{3,2,1,0:T(8,128)(2,1)} all-to-all(bf16[16,6,128,128]{3,2,1,0:T(8,128)(2,1)} %get-tuple-element.5.after), channel_id=1, replica_groups=mesh['fsdp'=16,'seq'=16] {'seq'}, dimensions={0} | all-to-all | bytes 6291456 | tf_op jit(solution)/shard_map/all_to_all | solution.py:204
  95.2 10.2 %all-to-all-start = ((bf16[16,6,128,128]{3,2,1,0:T(8,128)(2,1)}), bf16[16,6,128,128]{3,2,1,0:T(8,128)(2,1)S(1)}, u32[]{:S(2)}, u32[]{:S(2)}) async-start(bf16[16,6,128,128]{3,2,1,0:T(8,128)(2,1)} %get-tuple-element.4), calls=%async_computation | async-start | bytes 6291456 | tf_op jit(solution)/shard_map/all_to_all | solution.py:204
  106.1 1.5 shard_map.114
  109.0 0.8 bitcast_add_fusion
  111.4 1.1 collective-permute-done.6
  112.6 1.9 copy-done.2
  114.5 10.0 %shard_map.116 = bf16[16,2,128,128]{3,2,1,0:T(8,128)(2,1)S(1)} custom-call(s32[1,2]{1,0:T(1,128)S(1)} %copy-done.4, bf16[16,6,128,128]{3,2,1,0:T(8,128)(2,1)S(1)} %copy-done.2, f32[4,128]{1,0:T(4,128)S(1)} %bitcast.34), custom_call_target="tpu_custom_call" | custom-call | flops 4294967296 | bytes 4194304 | tf_op jit(solution)/shard_map/pallas_call | solution.py:188
  124.5 1.0 copy-done.3
  125.5 36.8 %all-to-all-done.in_ref = bf16[16,6,128,128]{3,2,1,0:T(8,128)(2,1)S(1)} async-done(((bf16[16,6,128,128]{3,2,1,0:T(8,128)(2,1)}), bf16[16,6,128,128]{3,2,1,0:T(8,128)(2,1)S(1)}, u32[]{:S(2)}, u32[]{:S(2)}) %all-to-all-start) | async-done | bytes 3145760 | tf_op jit(solution)/shard_map/all_to_all | solution.py:204
  162.2 1.6 copy-done
  163.9 3.8 %all-to-all-start.3 = ((bf16[16,2,128,128]{3,2,1,0:T(8,128)(2,1)}), bf16[16,2,128,128]{3,2,1,0:T(8,128)(2,1)S(1)}, u32[]{:S(2)}, u32[]{:S(2)}) async-start(bf16[16,2,128,128]{3,2,1,0:T(8,128)(2,1)} %copy-done.3), calls=%async_computation.3 | async-start | bytes 2097152 | tf_op jit(solution)/shard_map/all_to_all | solution.py:204
  167.7 1.9 copy-done.1
  169.6 9.7 %shard_map.115 = bf16[16,2,128,128]{3,2,1,0:T(8,128)(2,1)S(1)} custom-call(s32[1,2]{1,0:T(1,128)S(1)} %copy-done.4, bf16[16,6,128,128]{3,2,1,0:T(8,128)(2,1)S(1)} %copy-done.1, f32[4,128]{1,0:T(4,128)S(1)} %bitcast.33), custom_call_target="tpu_custom_call" | custom-call | flops 4294967296 | bytes 4194304 | tf_op jit(solution)/shard_map/pallas_call | solution.py:188
  179.3 6.5 %all-to-all-done.3.refs_1_ = bf16[16,2,128,128]{3,2,1,0:T(8,128)(2,1)S(1)} async-done(((bf16[16,2,128,128]{3,2,1,0:T(8,128)(2,1)}), bf16[16,2,128,128]{3,2,1,0:T(8,128)(2,1)S(1)}, u32[]{:S(2)}, u32[]{:S(2)}) %all-to-all-start.3) | async-done | bytes 1048608 | tf_op jit(solution)/shard_map/all_to_all | solution.py:204
  185.9 26.1 %all_to_all.21.refs_0_ = bf16[16,2,128,128]{3,2,1,0:T(8,128)(2,1)S(1)} all-to-all(bf16[16,2,128,128]{3,2,1,0:T(8,128)(2,1)S(1)} %shard_map.115), channel_id=1, replica_groups=mesh['fsdp'=16,'seq'=16] {'seq'}, dimensions={0} | all-to-all | bytes 2097152 | tf_op jit(solution)/shard_map/all_to_all | solution.py:204
  212.0 1.6 shard_map.117
  (40 shorter events, 5.4 us)
Async XLA Ops:
  2.7 6.2 %collective-permute-start = (f32[8,1024]{1,0:T(8,128)S(1)}, f32[8,1024]{1,0:T(8,128)S(1)}, u32[]{:S(2)}, u32[]{:S(2)}) collective-permute-start(f32[8,1024]{1,0:T(8,128)S(1)} %dynamic-slice_bitcast_fusion.1), channel_id=1, source_target_pairs={{16,144},{48,176},{80,208},{112,240},{144,16},{176,48},{208,80},{2... | collective-permute-start | bytes 98312 | tf_op jit(solution)/shard_map/ppermute | solution.py:245
  8.9 6.0 %collective-permute-start.1 = (f32[4,1024]{1,0:T(4,128)S(1)}, f32[4,1024]{1,0:T(4,128)S(1)}, u32[]{:S(2)}, u32[]{:S(2)}) collective-permute-start(f32[4,1024]{1,0:T(4,128)S(1)} %dynamic-slice_bitcast_fusion.3), channel_id=1, source_target_pairs={{16,80},{48,112},{80,16},{112,48},{144,208},{176,240},{208,144},{2... | collective-permute-start | bytes 49160 | tf_op jit(solution)/shard_map/ppermute | solution.py:245
  14.9 4.4 %collective-permute-start.2 = (f32[2,1024]{1,0:T(2,128)S(1)}, f32[2,1024]{1,0:T(2,128)S(1)}, u32[]{:S(2)}, u32[]{:S(2)}) collective-permute-start(f32[2,1024]{1,0:T(2,128)S(1)} %dynamic-slice_bitcast_fusion.5), channel_id=1, source_target_pairs={{16,48},{48,16},{80,112},{112,80},{144,176},{176,144},{208,240},{2... | collective-permute-start | bytes 24584 | tf_op jit(solution)/shard_map/ppermute | solution.py:245
  95.2 67.0 %all-to-all-start = ((bf16[16,6,128,128]{3,2,1,0:T(8,128)(2,1)}), bf16[16,6,128,128]{3,2,1,0:T(8,128)(2,1)S(1)}, u32[]{:S(2)}, u32[]{:S(2)}) async-start(bf16[16,6,128,128]{3,2,1,0:T(8,128)(2,1)} %get-tuple-element.4), calls=%async_computation | async-start | bytes 6291456 | tf_op jit(solution)/shard_map/all_to_all | solution.py:204
  105.4 5.8 %copy-start.5 = (f32[2,1024]{1,0:T(2,128)S(1)}, f32[2,1024]{1,0:T(2,128)}, u32[]{:S(2)}) copy-start(f32[2,1024]{1,0:T(2,128)} %bitcast_add_fusion.5.refs_6_) | copy-start | bytes 24580
  105.4 7.2 %copy-start.4 = (s32[1,2]{1,0:T(1,128)S(1)}, s32[1,2]{1,0:T(1,128)}, u32[]{:S(2)}) copy-start(s32[1,2]{1,0:T(1,128)} %len_ref.3) | copy-start | bytes 28
  108.3 0.7 collective-permute-start.3
  109.8 0.7 collective-permute-start.4
  110.6 0.7 collective-permute-start.5
  111.3 1.3 collective-permute-start.6
  112.6 1.9 copy-start.2
  124.5 1.0 copy-start.3
  162.2 1.6 copy-start
  163.9 22.0 %all-to-all-start.3 = ((bf16[16,2,128,128]{3,2,1,0:T(8,128)(2,1)}), bf16[16,2,128,128]{3,2,1,0:T(8,128)(2,1)S(1)}, u32[]{:S(2)}, u32[]{:S(2)}) async-start(bf16[16,2,128,128]{3,2,1,0:T(8,128)(2,1)} %copy-done.3), calls=%async_computation.3 | async-start | bytes 2097152 | tf_op jit(solution)/shard_map/all_to_all | solution.py:204
  167.7 1.9 copy-start.1
